TPU v7x, 512 devices: a whole 4x8x8 slice. The times are simulated.
512 devices in a mesh: trc: 8 (over y_lo, core), ty: 4 (over x), tx: 16 (over z, y_hi).
Axes of the slice: x: 4, y: 8 (y_hi: 2, y_lo: 4; y = y_hi * 4 + y_lo), z: 8, core: 2. Of those that a mesh axis runs over, the one named last changes fastest.
Arguments:
- tracers: float32 [80, 8, 64, 2048], P('trc', None, 'ty', 'tx'), may hold values from -6 to 6
- courant: float32 [2, 8, 64, 2048], P(None, 'trc', 'ty', 'tx'), may hold values from -0.9 to 0.9
- assignment: int32 [80], replicated, may hold values from 0 to 79, each once
- species_gain: float32 [80], replicated, may hold values from 0.3 to 3
- w_in: bfloat16 [256, 80], replicated, may hold values from -0.625 to 0.625
- b_in: float32 [256], replicated, may hold values from -3 to 3
- w_mid: bfloat16 [2, 256, 256], replicated, may hold values from -0.375 to 0.375
- b_mid: float32 [2, 256], replicated, may hold values from -3 to 3
- w_out: bfloat16 [80, 256], replicated, may hold values from -0.375 to 0.375
- b_out: float32 [80], replicated, may hold values from -3 to 3
Outputs:
- updated: float32 [80, 8, 64, 2048], P('trc', None, 'ty', 'tx')
Inputs may be any that keep to these rules, and one draw needn't show every extreme that they name: `assignment`: each species stands in exactly one tracer slot.
All inputs are finite; a program needn't handle non-finite values.
Results may differ from a plain program's by a relative error of at most 0.0029.
Values sent between devices are 32-bit elements; how exact they have to be, the bound alone decides.
A program may use at most 64 MiB of HBM per device.

v0:
```python
import jax
import jax.numpy as jnp
from jax import lax
from jax.sharding import PartitionSpec as P

MIDL = 2


def extended(value, sides, width, wrap):
    for axis, dim in sides:
        size, length = (lax.axis_size(axis), value.shape[dim])
        up = [(i, (i + 1) % size) for i in range(size if wrap else size - 1)]
        down = [(j, i) for i, j in up]
        last = lax.slice_in_dim(value, length - width, length, axis=dim)
        initial = lax.slice_in_dim(value, 0, width, axis=dim)
        before = lax.ppermute(last, axis, up)
        after = lax.ppermute(initial, axis, down)
        value = jnp.concatenate([before, value, after], axis=dim)
    return value


def cut_range(values, begin_at, end_at, along):
    return lax.slice_in_dim(values, begin_at, end_at, axis=along)


def parabolic_sweep(padded, speeds, along):
    count = padded.shape[along] - 6
    edge_values = 7.0 / 12.0 * (
        cut_range(padded, 1, count + 4, along) + cut_range(padded, 2, count + 5, along)
    ) - 1.0 / 12.0 * (
        cut_range(padded, 0, count + 3, along) + cut_range(padded, 3, count + 6, along)
    )
    left_edge = cut_range(edge_values, 0, count + 2, along)
    right_edge = cut_range(edge_values, 1, count + 3, along)
    centre = cut_range(padded, 2, count + 4, along)
    edge_slope = right_edge - left_edge
    curvature = 6.0 * (centre - 0.5 * (left_edge + right_edge))
    face_speed = 0.5 * (
        cut_range(speeds, 2, count + 3, along) + cut_range(speeds, 3, count + 4, along)
    )
    from_left = face_speed * (
        cut_range(right_edge, 0, count + 1, along)
        - 0.5
        * face_speed
        * (
            cut_range(edge_slope, 0, count + 1, along)
            - (1.0 - face_speed * (2.0 / 3.0)) * cut_range(curvature, 0, count + 1, along)
        )
    )
    from_right = face_speed * (
        cut_range(left_edge, 1, count + 2, along)
        - 0.5
        * face_speed
        * (
            cut_range(edge_slope, 1, count + 2, along)
            + (1.0 + face_speed * (2.0 / 3.0)) * cut_range(curvature, 1, count + 2, along)
        )
    )
    face_flux = jnp.where(face_speed > 0.0, from_left, from_right)
    return cut_range(padded, 3, count + 3, along) - (
        cut_range(face_flux, 1, count + 1, along) - cut_range(face_flux, 0, count, along)
    )


def advect(tracer_field, wind_field):
    species = tracer_field.shape[0]
    stacked = jnp.concatenate([tracer_field, wind_field], axis=0)
    padded_cols = extended(stacked, (("tx", 3),), 3, True)
    swept = parabolic_sweep(padded_cols[:species], padded_cols[species : species + 1], 3)
    restacked = jnp.concatenate([swept, wind_field], axis=0)
    padded_rows = extended(restacked, (("ty", 2),), 3, False)
    tracer_field = parabolic_sweep(padded_rows[:species], padded_rows[species + 1 : species + 2], 2)
    return tracer_field


def local(tracers, courant, assignment, species_gain, w_in, b_in, w_mid, b_mid, w_out, b_out):
    gain_slot = jnp.take(species_gain, assignment)
    w_first = jnp.take(w_in, assignment, axis=1)
    w_last = jnp.take(w_out, assignment, axis=0)
    b_last = jnp.take(b_out, assignment)
    local_species, levels, tile_rows, tile_cols = tracers.shape
    wind_field = lax.all_gather(courant, "trc", axis=1, tiled=True)
    advected = advect(tracers, wind_field)
    by_cells = advected.reshape(local_species, levels, tile_rows * tile_cols)
    cell_block = lax.all_to_all(by_cells, "trc", split_axis=2, concat_axis=0, tiled=True)
    scaled = (cell_block * gain_slot[:, None, None]).astype(jnp.bfloat16)
    hidden = jax.nn.gelu(
        jnp.einsum("hs,skm->hkm", w_first, scaled, preferred_element_type=jnp.float32)
        + b_in[:, None, None]
    ).astype(jnp.bfloat16)
    for mid_layer in range(MIDL):
        hidden = jax.nn.gelu(
            jnp.einsum("hg,gkm->hkm", w_mid[mid_layer], hidden, preferred_element_type=jnp.float32)
            + b_mid[mid_layer][:, None, None]
        ).astype(jnp.bfloat16)
    tendency = (
        jnp.einsum("sh,hkm->skm", w_last, hidden, preferred_element_type=jnp.float32)
        + b_last[:, None, None]
    )
    result = cell_block + tendency
    returned = lax.all_to_all(result, "trc", split_axis=0, concat_axis=2, tiled=True)
    return returned.reshape(local_species, levels, tile_rows, tile_cols)


def solution(mesh):
    in_specs = (
        P("trc", None, "ty", "tx"),
        P(None, "trc", "ty", "tx"),
        P(),
        P(),
        P(),
        P(),
        P(),
        P(),
        P(),
        P(),
    )
    out_specs = P("trc", None, "ty", "tx")
    return jax.shard_map(local, mesh=mesh, in_specs=in_specs, out_specs=out_specs, check_vma=False)
```

profile of v0, /device:TPU:1, one launch (start us, length us, event | category | flops | bytes accessed | tf_op | source)
XLA Modules:
  0.0 140.9 jit_solution(11289169647425792354)
XLA Ops:
  0.0 1.2 constant_dynamic-update-slice_fusion.1
  1.2 20.7 %all_gather.3 = f32[2,8,16,128]{3,2,0,1:T(8,128)S(1)} all-gather(f32[2,1,16,128]{3,2,0,1:T(8,128)S(1)} %bitcast.64), channel_id=1, replica_groups=mesh['trc'=8,'ty'=4,'tx'=16] {'trc'}, dimensions={1}, use_global_device_ids=true | all-gather | bytes 147456 | tf_op jit(solution)/shard_map/all_gather | solution.py:82
  22.8 2.1 %collective-permute-start = (f32[12,8,16,3]{2,1,3,0:T(8,128)S(1)}, f32[12,8,16,3]{2,1,3,0:T(8,128)S(1)}, u32[]{:S(2)}, u32[]{:S(2)}) collective-permute-start(f32[12,8,16,3]{2,1,3,0:T(8,128)S(1)} %copy.154), channel_id=1, source_target_pairs={{0,1},{1,2},{2,3},{3,4},{4,5},{5,6},{6,7},{7,8},{8,9},{9,10},{10,1... | collective-permute-start | bytes 55304 | tf_op jit(solution)/shard_map/ppermute | solution.py:16
  25.5 10.4 %collective-permute-start.1 = (f32[12,8,16,3]{2,1,3,0:T(8,128)S(1)}, f32[12,8,16,3]{2,1,3,0:T(8,128)S(1)}, u32[]{:S(2)}, u32[]{:S(2)}) collective-permute-start(f32[12,8,16,3]{2,1,3,0:T(8,128)S(1)} %copy.156), channel_id=1, source_target_pairs={{1,0},{2,1},{3,2},{4,3},{5,4},{6,5},{7,6},{8,7},{9,8},{10,9},{11,1... | collective-permute-start | bytes 55304 | tf_op jit(solution)/shard_map/ppermute | solution.py:17
  36.0 1.6 %collective-permute-done = f32[12,8,16,3]{2,1,3,0:T(8,128)S(1)} collective-permute-done((f32[12,8,16,3]{2,1,3,0:T(8,128)S(1)}, f32[12,8,16,3]{2,1,3,0:T(8,128)S(1)}, u32[]{:S(2)}, u32[]{:S(2)}) %collective-permute-start) | collective-permute-done | bytes 18464 | tf_op jit(solution)/shard_map/ppermute | solution.py:16
  38.1 3.7 %collective-permute-done.1 = f32[12,8,16,3]{2,1,3,0:T(8,128)S(1)} collective-permute-done((f32[12,8,16,3]{2,1,3,0:T(8,128)S(1)}, f32[12,8,16,3]{2,1,3,0:T(8,128)S(1)}, u32[]{:S(2)}, u32[]{:S(2)}) %collective-permute-start.1) | collective-permute-done | bytes 18464 | tf_op jit(solution)/shard_map/ppermute | solution.py:17
  43.3 1.1 fusion.36
  45.2 1.1 fusion.28
  46.7 3.1 %collective-permute-start.2 = (f32[12,8,3,128]{3,1,2,0:T(8,128)S(1)}, f32[12,8,3,128]{3,1,2,0:T(8,128)S(1)}, u32[]{:S(2)}, u32[]{:S(2)}) collective-permute-start(f32[12,8,3,128]{3,1,2,0:T(8,128)S(1)} %copy.161), channel_id=1, source_target_pairs={{0,16},{16,32},{32,48},{1,17},{17,33},{33,49},{2,18},{18,34},{34,5... | collective-permute-start | bytes 442376 | tf_op jit(solution)/shard_map/ppermute | solution.py:16
  49.8 1.3 collective-permute-start.3
  51.1 1.1 collective-permute-done.2
  52.3 3.8 %collective-permute-done.3 = f32[12,8,3,128]{3,1,2,0:T(8,128)S(1)} collective-permute-done((f32[12,8,3,128]{3,1,2,0:T(8,128)S(1)}, f32[12,8,3,128]{3,1,2,0:T(8,128)S(1)}, u32[]{:S(2)}, u32[]{:S(2)}) %collective-permute-start.3) | collective-permute-done | bytes 147488 | tf_op jit(solution)/shard_map/ppermute | solution.py:17
  57.9 4.6 %copy.182 = f32[10,8,16,128]{0,1,3,2:T(8,128)} copy(f32[10,8,16,128]{3,2,1,0:T(8,128)S(1)} %fusion.58) | data formatting | bytes 1310720 | tf_op jit(solution)/shard_map/reshape | solution.py:84
  62.5 9.5 %reshape.68 = f32[8,1,20480]{2,1,0:T(1,128)} reshape(f32[2048,8,10]{2,1,0:T(8,128)} %bitcast.60) | data formatting | bytes 1310720
  71.9 5.5 %all-to-all-start = ((f32[8,1,20480]{2,1,0:T(1,128)}), f32[8,1,20480]{2,1,0:T(1,128)S(1)}, u32[]{:S(2)}, u32[]{:S(2)}) async-start(f32[8,1,20480]{2,1,0:T(1,128)} %reshape.68), calls=%async_computation | async-start | bytes 1310720 | tf_op jit(solution)/shard_map/all_to_all | solution.py:85
  77.5 1.2 gather_fusion.3
  78.7 1.2 gather_fusion.2
  81.5 13.3 %all-to-all-done = f32[8,1,20480]{2,1,0:T(1,128)S(1)} async-done(((f32[8,1,20480]{2,1,0:T(1,128)}), f32[8,1,20480]{2,1,0:T(1,128)S(1)}, u32[]{:S(2)}, u32[]{:S(2)}) %all-to-all-start) | async-done | bytes 655392 | tf_op jit(solution)/shard_map/all_to_all | solution.py:85
  95.3 2.3 %reduce = f32[8,20480]{1,0:T(8,128)S(1)} reduce(f32[8,1,20480]{2,1,0:T(1,128)S(1)} %all-to-all-done, f32[]{:T(128)} %broadcast.89), dimensions={1}, to_apply=%all_to_all.24.reduce_sub_computation | reduce | bytes 1310724 | tf_op jit(solution)/shard_map/all_to_all | solution.py:85
  97.6 12.5 %reshape.69 = f32[2048,8,10]{2,1,0:T(8,128)} reshape(f32[8,20480]{1,0:T(8,128)S(1)} %reduce) | data formatting | bytes 1310720
  110.0 5.3 %copy.169 = f32[8,10,8,256]{3,2,1,0:T(8,128)S(1)} copy(f32[8,10,8,256]{1,2,3,0:T(8,128)} %bitcast.61) | data formatting | bytes 1310720 | tf_op jit(solution)/shard_map/all_to_all | solution.py:85
  115.5 1.0 fusion.7
  116.5 1.7 %fusion.23 = bf16[256,8,256]{2,0,1:T(8,128)(2,1)S(1)} fusion(bf16[256,8,256]{2,0,1:T(8,128)(2,1)S(1)} %fusion.7, f32[256]{0:T(256)S(1)} %bitcast.66, f32[256]{0:T(256)S(1)} %bitcast.65, bf16[2,256,256]{2,1,0:T(8,128)(2,1)S(1)} %copy-done.8), kind=kOutput, calls=%fused_computation.30 | convolution fusion | flops 547356672 | bytes 2361344 | tf_op jit(solution)/shard_map/hg,gkm->hkm/dot_general | solution.py:93
  119.0 20.6 %all_to_all.33 = f32[80,8,256]{2,1,0:T(8,128)S(1)} all-to-all(f32[80,8,256]{2,1,0:T(8,128)S(1)} %copy.176), channel_id=1, replica_groups=mesh['trc'=8,'ty'=4,'tx'=16] {'trc'}, dimensions={0} | all-to-all | bytes 1310720 | tf_op jit(solution)/shard_map/all_to_all | solution.py:101
  (56 shorter events, 10.9 us)
Async XLA Ops:
  0.0 80.0 %copy-start = (bf16[256,80]{0,1:T(8,128)(2,1)S(1)}, bf16[256,80]{0,1:T(8,128)(2,1)}, u32[]{:S(2)}) copy-start(bf16[256,80]{0,1:T(8,128)(2,1)} %param.16) | copy-start | bytes 122884
  0.0 1.2 copy-start.5
  22.8 14.7 %collective-permute-start = (f32[12,8,16,3]{2,1,3,0:T(8,128)S(1)}, f32[12,8,16,3]{2,1,3,0:T(8,128)S(1)}, u32[]{:S(2)}, u32[]{:S(2)}) collective-permute-start(f32[12,8,16,3]{2,1,3,0:T(8,128)S(1)} %copy.154), channel_id=1, source_target_pairs={{0,1},{1,2},{2,3},{3,4},{4,5},{5,6},{6,7},{7,8},{8,9},{9,10},{10,1... | collective-permute-start | bytes 55304 | tf_op jit(solution)/shard_map/ppermute | solution.py:16
  25.5 16.3 %collective-permute-start.1 = (f32[12,8,16,3]{2,1,3,0:T(8,128)S(1)}, f32[12,8,16,3]{2,1,3,0:T(8,128)S(1)}, u32[]{:S(2)}, u32[]{:S(2)}) collective-permute-start(f32[12,8,16,3]{2,1,3,0:T(8,128)S(1)} %copy.156), channel_id=1, source_target_pairs={{1,0},{2,1},{3,2},{4,3},{5,4},{6,5},{7,6},{8,7},{9,8},{10,9},{11,1... | collective-permute-start | bytes 55304 | tf_op jit(solution)/shard_map/ppermute | solution.py:17
  45.2 1.1 copy-start.3
  46.7 5.6 %collective-permute-start.2 = (f32[12,8,3,128]{3,1,2,0:T(8,128)S(1)}, f32[12,8,3,128]{3,1,2,0:T(8,128)S(1)}, u32[]{:S(2)}, u32[]{:S(2)}) collective-permute-start(f32[12,8,3,128]{3,1,2,0:T(8,128)S(1)} %copy.161), channel_id=1, source_target_pairs={{0,16},{16,32},{32,48},{1,17},{17,33},{33,49},{2,18},{18,34},{34,5... | collective-permute-start | bytes 442376 | tf_op jit(solution)/shard_map/ppermute | solution.py:16
  49.8 6.2 %collective-permute-start.3 = (f32[12,8,3,128]{3,1,2,0:T(8,128)S(1)}, f32[12,8,3,128]{3,1,2,0:T(8,128)S(1)}, u32[]{:S(2)}, u32[]{:S(2)}) collective-permute-start(f32[12,8,3,128]{3,1,2,0:T(8,128)S(1)} %copy.163), channel_id=1, source_target_pairs={{16,0},{32,16},{48,32},{17,1},{33,17},{49,33},{18,2},{34,18},{50,3... | collective-permute-start | bytes 442376 | tf_op jit(solution)/shard_map/ppermute | solution.py:17
  71.9 5.5 %copy-start.7 = (s32[80]{0:T(128)S(1)}, s32[80]{0:T(128)}, u32[]{:S(2)}) copy-start(s32[80]{0:T(128)} %param.14) | copy-start | bytes 964
  71.9 5.6 %copy-start.1 = (f32[80]{0:T(128)S(1)}, f32[80]{0:T(128)}, u32[]{:S(2)}) copy-start(f32[80]{0:T(128)} %param.21) | copy-start | bytes 964
  71.9 6.8 %copy-start.2 = (f32[80]{0:T(128)S(1)}, f32[80]{0:T(128)}, u32[]{:S(2)}) copy-start(f32[80]{0:T(128)} %param.15) | copy-start | bytes 964
  71.9 8.8 %copy-start.4 = (bf16[80,256]{1,0:T(8,128)(2,1)S(1)}, bf16[80,256]{1,0:T(8,128)(2,1)}, u32[]{:S(2)}) copy-start(bf16[80,256]{1,0:T(8,128)(2,1)} %param.20) | copy-start | bytes 122884
  71.9 22.8 %all-to-all-start = ((f32[8,1,20480]{2,1,0:T(1,128)}), f32[8,1,20480]{2,1,0:T(1,128)S(1)}, u32[]{:S(2)}, u32[]{:S(2)}) async-start(f32[8,1,20480]{2,1,0:T(1,128)} %reshape.68), calls=%async_computation | async-start | bytes 1310720 | tf_op jit(solution)/shard_map/all_to_all | solution.py:85
  77.4 4.0 %copy-start.6 = (f32[2,256]{1,0:T(2,128)S(1)}, f32[2,256]{1,0:T(2,128)}, u32[]{:S(2)}) copy-start(f32[2,256]{1,0:T(2,128)} %param.19) | copy-start | bytes 6148
  110.0 5.4 %copy-start.9 = (f32[256]{0:T(256)S(1)}, f32[256]{0:T(256)}, u32[]{:S(2)}) copy-start(f32[256]{0:T(256)} %param.17) | copy-start | bytes 3076
  115.4 1.0 copy-start.8
where the time goes:
time: 141 us
  local copies, waits for them, and re-layouts  42 us (30%)
  blocking collectives  41.3 us (29%)
  waiting for transfers between devices  23.4 us (17%)
  starting transfers between devices  22.4 us (16%)
  other arithmetic  8.27 us (6%)
  matrix products  3.13 us (2%)
    unnamed x23, local copies, waits for them, and re-layouts  23.1 us
    all_gather x1, blocking collectives, local(): wind_field = lax.all_gather(courant, 'trc', axis=1, tiled=True)  20.7 us
    all_to_all x1, blocking collectives, local(): lax.all_to_all(result, 'trc', split_axis=0, concat_axis=2, tiled=True)  20.6 us
    all_to_all x1, waiting for transfers between devices, local(): lax.all_to_all(by_cells, 'trc', split_axis=2, concat_axis=0, tiled=True)  13.3 us
    ppermute x2, starting transfers between devices, extended(): after = lax.ppermute(initial, axis, down)  11.7 us
    ppermute x2, waiting for transfers between devices, extended(): after = lax.ppermute(initial, axis, down)  7.49 us
    all_to_all x2, local copies, waits for them, and re-layouts, local(): lax.all_to_all(by_cells, 'trc', split_axis=2, concat_axis=0, tiled=True)  5.77 us
    all_to_all x1, starting transfers between devices, local(): lax.all_to_all(by_cells, 'trc', split_axis=2, concat_axis=0, tiled=True)  5.51 us
  transfers between devices with their start and end apart: 5, of which 5 were waited for; matrix products, arithmetic and copies ran while one was open for 4% of the time, Pallas kernels for 0%

commit v1 on v0

v1 whole, which is shorter than its diff:
```python
import functools

import jax
import jax.numpy as jnp
from jax import lax
from jax.experimental import pallas as pl
from jax.experimental.pallas import tpu as pltpu
from jax.sharding import PartitionSpec as P

MESH = pl.DeviceIdType.MESH
GROUPS = (5, 4, 4, 3)
STARTS_EVEN = (11, 7, 3, 0)
STARTS_ODD = (0, 5, 9, 13)


def upwind(f):
    up, down = jnp.maximum(f, 0.0), jnp.minimum(f, 0.0)
    p2, m2 = 0.5 * up * up, 0.5 * down * down
    return up, p2, p2 * (1.0 - (2.0 / 3.0) * up), down, m2, m2 * (1.0 + (2.0 / 3.0) * down)


def edge(a, b, c, d):
    return (7.0 / 12.0) * (b + c) - (1.0 / 12.0) * (a + d)


def sweep_lanes(q, coef):
    p1, p2, p3, m1, m2, m3 = coef
    left = edge(pltpu.roll(q, 2, 1), pltpu.roll(q, 1, 1), q, pltpu.roll(q, 127, 1))
    right = pltpu.roll(left, 127, 1)
    slope = right - left
    curve = 6.0 * q - 3.0 * (left + right)
    out_right = p1 * right - p2 * slope + p3 * curve
    out_left = m1 * left - m2 * slope - m3 * curve
    return q - out_right + out_left + pltpu.roll(out_right, 1, 1) - pltpu.roll(out_left, 127, 1)


def gelu(v):
    inner = v * (0.7978845608028654 + (0.7978845608028654 * 0.044715) * (v * v))
    half = 0.5 * v
    return (half + half * jnp.tanh(inner)).astype(jnp.bfloat16)


def column_of(row, size):
    at = lax.broadcasted_iota(jnp.int32, (size, size), 0)
    to = lax.broadcasted_iota(jnp.int32, (size, size), 1)
    return jnp.sum(jnp.where(at == to, row, 0.0), axis=1, keepdims=True)


def kernel(
    x_ref, c_ref, as_ref, gain_ref, win_ref, bin_ref, wmid_ref, bmid_ref, wout_ref, bout_ref,
    o_ref,
    got, swept, strip, fixed, adv, back, cv, c1h, eco, ecl, ecr, t_out, t_in, cc, cf, sc,
    v_as, v_gain, v_win, v_bin, v_wmid, v_bmid, v_wout, v_bout,
    first_w, last_w, bias_b, last_b, gain_b,
    fs, fr, fl, lw, ts, tr, es, er, c1s, c1r, hs, hr, os_, or_, ol,
):
    me, y, x = lax.axis_index("trc"), lax.axis_index("ty"), lax.axis_index("tx")
    even = 1 - lax.rem(y, 2)
    left, right = {"tx": lax.rem(x + 15, 16)}, {"tx": lax.rem(x + 1, 16)}

    def remote(src, dst, send, recv, to):
        return pltpu.make_async_remote_copy(src, dst, send, recv, device_id=to, device_id_type=MESH)

    def peer(d):
        return lax.rem(me + d, 8)

    loads = [
        pltpu.make_async_copy(src, dst, lw.at[i])
        for i, (src, dst) in enumerate((
            (c_ref.at[:, 0], cv), (as_ref, v_as), (gain_ref, v_gain), (win_ref, v_win), (bin_ref, v_bin),
            (wmid_ref, v_wmid), (bmid_ref, v_bmid), (wout_ref, v_wout), (bout_ref, v_bout),
        ))
    ]
    for load in loads:
        load.start()

    c1h[...] = jnp.zeros((2, 8, 128), jnp.float32)
    barrier = pltpu.get_barrier_semaphore()
    for d in range(1, 8):
        pl.semaphore_signal(barrier, inc=1, device_id={"trc": peer(d)}, device_id_type=MESH)
    for to in (left, right, {"ty": lax.rem(y + 3, 4)}, {"ty": lax.rem(y + 1, 4)}):
        pl.semaphore_signal(barrier, inc=1, device_id=to, device_id_type=MESH)

    lane8 = lax.broadcasted_iota(jnp.int32, (8, 128), 1)
    lane16 = lax.broadcasted_iota(jnp.int32, (16, 128), 1)
    row16 = lax.broadcasted_iota(jnp.int32, (16, 128), 0)

    loads[0].wait()
    c0 = cv[0]
    wind = jnp.zeros((16, 128), jnp.float32)
    for i in range(8):
        wind = jnp.where((lane16 // 16 == i) & (row16 % 8 == i), pltpu.roll(c0, (16 * i + 8) % 128, 1), wind)
    eco[...] = jnp.zeros((8, 128), jnp.float32)
    eco[0:1, :] = jnp.sum(wind[0:8], axis=0, keepdims=True)
    eco[1:2, :] = jnp.sum(wind[8:16], axis=0, keepdims=True)

    @pl.when(y == 0)
    def _():
        swept[0:3] = jnp.zeros((3, 80, 128), jnp.float32)

    @pl.when(y == 3)
    def _():
        swept[19:22] = jnp.zeros((3, 80, 128), jnp.float32)

    pl.semaphore_wait(barrier, 11)

    ec_copies = (remote(eco, ecr, es.at[0], er.at[0], left), remote(eco, ecl, es.at[1], er.at[1], right))
    for copy in ec_copies:
        copy.start()
    wind_up = remote(cv.at[1, pl.ds(0, 1)], c1h.at[1, pl.ds(0, 1)], c1s.at[0], c1r.at[0], {"ty": y - 1})
    wind_down = remote(cv.at[1, pl.ds(15, 1)], c1h.at[0, pl.ds(0, 1)], c1s.at[1], c1r.at[1], {"ty": y + 1})

    @pl.when(y > 0)
    def _():
        wind_up.start()

    @pl.when(y < 3)
    def _():
        wind_down.start()

    halves = (8 * even, 8 * (1 - even))

    def forward(p, d):
        k = peer(d)
        rows = pl.ds(pl.multiple_of(halves[p], 8), 8)
        return remote(
            x_ref.at[:, k, rows], got.at[p, pl.ds(10 * me, 10)], fs.at[p, k], fr.at[p, me], {"trc": k}
        )

    def arriving(p, d):
        k = peer(d)
        there = got.at[p, pl.ds(10 * k, 10)]
        return remote(there, there, fs.at[p, k], fr.at[p, k], {"trc": k})

    def own(p):
        rows = pl.ds(pl.multiple_of(halves[p], 8), 8)
        return pltpu.make_async_copy(x_ref.at[:, me, rows], got.at[p, pl.ds(10 * me, 10)], fl.at[p])

    for p in range(2):
        for d in range(1, 8):
            forward(p, d).start()
        own(p).start()

    for load in loads[1:]:
        load.wait()
    species = lax.broadcasted_iota(jnp.int32, (80, 80), 1)
    held = column_of(v_as[...].astype(jnp.float32), 80).astype(jnp.int32)
    chosen = held == species
    pick = jnp.where(chosen, 1.0, 0.0).astype(jnp.bfloat16)
    first_w[...] = lax.dot_general(
        v_win[...], pick, (((1,), (1,)), ((), ())), preferred_element_type=jnp.float32
    ).astype(jnp.bfloat16)
    last_w[...] = jnp.dot(pick, v_wout[...], preferred_element_type=jnp.float32).astype(jnp.bfloat16)
    gain_b[...] = jnp.broadcast_to(jnp.sum(jnp.where(chosen, v_gain[...], 0.0), axis=1, keepdims=True), (80, 128))
    last_b[...] = jnp.broadcast_to(jnp.sum(jnp.where(chosen, v_bout[...], 0.0), axis=1, keepdims=True), (80, 128))
    bias_b[0] = jnp.broadcast_to(column_of(v_bin[...], 256), (256, 128))
    bias_b[1] = jnp.broadcast_to(column_of(v_bmid[0:1, :], 256), (256, 128))
    bias_b[2] = jnp.broadcast_to(column_of(v_bmid[1:2, :], 256), (256, 128))

    at_left = 0.5 * (pltpu.roll(c0, 1, 1) + c0)
    at_right = pltpu.roll(at_left, 127, 1)
    coef = upwind(at_right)[:3] + upwind(at_left)[3:]
    for i in range(6):
        cc[:, i, :] = coef[i]

    for copy in ec_copies:
        copy.wait()
    inner = lane8 % 16 < 8
    for side, wind8 in enumerate((jnp.where(inner, ecl[...], eco[...]), jnp.where(inner, eco[...], ecr[...]))):
        at_left = 0.5 * (pltpu.roll(wind8, 1, 1) + wind8)
        at_right = pltpu.roll(at_left, 127, 1)
        coef = upwind(at_right)[:3] + upwind(at_left)[3:]
        for i in range(6):
            sc[side, 0, i : i + 1, :] = coef[i][0:1]
            sc[side, 1, i : i + 1, :] = coef[i][1:2]

    @pl.when(y > 0)
    def _():
        wind_up.wait_send()
        wind_down.wait_recv()

    @pl.when(y < 3)
    def _():
        wind_down.wait_send()
        wind_up.wait_recv()

    c1 = cv[1]
    above = jnp.where(row16 == 0, c1h[0, 0:1, :], pltpu.roll(c1, 1, 0))
    coef = upwind(0.5 * (above + c1))
    for i in range(6):
        cf[0:16, i, :] = coef[i]
    coef = upwind(0.5 * (c1[15:16] + c1h[1, 0:1, :]))
    for i in range(6):
        cf[16, i : i + 1, :] = coef[i]

    got2 = [got.at[p].reshape(640, 128) for p in range(2)]
    back2 = [back.at[p].reshape(640, 128) for p in range(4)]

    def row_coef(ref, *at):
        return [ref[(*at, pl.ds(i, 1), slice(None))] for i in range(6)]

    def half(p):
        base = halves[p]
        for d in range(1, 8):
            arriving(p, d).wait_recv()
        own(p).wait()

        @pl.loop(0, 10)
        def _(g):
            e = jnp.zeros((8, 128), jnp.float32)
            for i in range(8):
                q = got2[p][pl.ds(g * 64 + i, 8, stride=8), :]
                e = jnp.where(lane8 // 16 == i, pltpu.roll(q, (16 * i + 8) % 128, 1), e)
            strip[p, pl.ds(pl.multiple_of(g * 8, 8), 8), :] = e

        for side, first in enumerate((8, 5)):
            for u in range(2):
                t = None
                for slot in range(5):
                    e = pltpu.roll(strip[p, 16 * slot + 8 * u : 16 * slot + 8 * u + 8, :], (3 * slot - first) % 128, 1)
                    t = e if t is None else jnp.where((lane8 % 16) // 3 == slot, e, t)
                t_out[p, side, 8 * u : 8 * u + 8, :] = t
        to_left = remote(t_out.at[p, 0], t_in.at[p, 1], ts.at[p, 0], tr.at[p, 1], left)
        to_right = remote(t_out.at[p, 1], t_in.at[p, 0], ts.at[p, 1], tr.at[p, 0], right)
        to_left.start()
        to_right.start()

        @pl.loop(0, 8)
        def _(i):
            coef = row_coef(cc, base + i)
            for g in range(0, 80, 16):
                q = got2[p][pl.ds(g * 8 + i, 16, stride=8), :]
                swept[base + i + 3, g : g + 16, :] = sweep_lanes(q, coef)

        to_left.wait()
        to_right.wait()
        coefs = [row_coef(sc, side, base // 8) for side in range(2)]
        for g in range(10):
            slot, u = g // 2, g % 2
            mine = strip[p, 8 * g : 8 * g + 8, :]
            before = pltpu.roll(t_in[p, 0, 8 * u : 8 * u + 8, :], (5 - 3 * slot) % 128, 1)
            after = pltpu.roll(t_in[p, 1, 8 * u : 8 * u + 8, :], (8 - 3 * slot) % 128, 1)
            new_left = sweep_lanes(jnp.where(inner, before, mine), coefs[0])
            new_right = sweep_lanes(jnp.where(inner, mine, after), coefs[1])
            fixed[8 * g : 8 * g + 8, :] = jnp.where(inner, new_right, new_left)
        sides = (lane8 < 3) | (lane8 >= 125)
        for i in range(8):
            for g in range(0, 80, 8):
                at = (base + i + 3, pl.ds(g, 8), slice(None))
                swept[at] = jnp.where(sides, pltpu.roll(fixed[g : g + 8, :], 120 - 16 * i, 1), swept[at])

    def rows_out(p):
        n = GROUPS[p]
        start = STARTS_ODD[p] + even * (STARTS_EVEN[p] - STARTS_ODD[p])

        @pl.loop(0, 10)
        def _(g):
            at = pl.ds(pl.multiple_of(g * 8, 8), 8)
            s = [swept[start + t, at, :] for t in range(n + 6)]
            e = [edge(*s[j : j + 4]) for j in range(n + 3)]
            flux = [None] * (n + 1)
            for j in range(n + 2):
                slope = e[j + 1] - e[j]
                curve = 6.0 * s[j + 2] - 3.0 * (e[j] + e[j + 1])
                if j <= n:
                    p1, p2, p3 = (cf[start + j, i : i + 1, :] for i in range(3))
                    flux[j] = p1 * e[j + 1] - p2 * slope + p3 * curve
                if j >= 1:
                    m1, m2, m3 = (cf[start + j - 1, i : i + 1, :] for i in range(3, 6))
                    flux[j - 1] = flux[j - 1] + (m1 * e[j] - m2 * slope - m3 * curve)
            for t in range(n):
                adv[t, at, :] = s[t + 3] - (flux[t + 1] - flux[t])

        wide = lambda v: jnp.concatenate([v] * n, axis=1)
        h = jnp.concatenate([(adv[t] * gain_b[...]).astype(jnp.bfloat16) for t in range(n)], axis=1)
        h = gelu(jnp.dot(first_w[...], h, preferred_element_type=jnp.float32) + wide(bias_b[0]))
        for m in range(2):
            h = gelu(jnp.dot(v_wmid[m], h, preferred_element_type=jnp.float32) + wide(bias_b[m + 1]))
        tend = jnp.dot(last_w[...], h, preferred_element_type=jnp.float32)
        for t in range(n):
            back2[p][pl.ds(t, 80, stride=8), :] = adv[t] + (tend[:, 128 * t : 128 * t + 128] + last_b[...])
        rows = pl.ds(start, n)
        for d in range(1, 8):
            k = peer(d)
            remote(
                back.at[p, pl.ds(10 * k, 10), pl.ds(0, n)], o_ref.at[:, me, rows], os_.at[p, k], or_.at[p, me], {"trc": k}
            ).start()
        pltpu.make_async_copy(back.at[p, pl.ds(10 * me, 10), pl.ds(0, n)], o_ref.at[:, me, rows], ol.at[p]).start()

    def finish(p):
        n = GROUPS[p]
        rows = pl.ds(STARTS_ODD[p] + even * (STARTS_EVEN[p] - STARTS_ODD[p]), n)
        for d in range(1, 8):
            k = peer(d)
            remote(
                back.at[p, pl.ds(10 * k, 10), pl.ds(0, n)], o_ref.at[:, k, rows], os_.at[p, k], or_.at[p, k], {"trc": k}
            ).wait()
        pltpu.make_async_copy(back.at[p, pl.ds(10 * me, 10), pl.ds(0, n)], o_ref.at[:, me, rows], ol.at[p]).wait()

    down = remote(swept.at[pl.ds(16, 3)], swept.at[pl.ds(0, 3)], hs.at[0], hr.at[0], {"ty": y + 1})
    up = remote(swept.at[pl.ds(3, 3)], swept.at[pl.ds(19, 3)], hs.at[1], hr.at[1], {"ty": y - 1})

    half(0)

    @pl.when(even == 1)
    def _():
        down.start()

    @pl.when(even == 0)
    def _():
        up.start()

    @pl.when(even == 1)
    def _():
        up.wait_recv()

    @pl.when(even == 0)
    def _():
        down.wait_recv()

    rows_out(0)
    half(1)

    @pl.when((even == 1) & (y > 0))
    def _():
        up.start()

    @pl.when((even == 0) & (y < 3))
    def _():
        down.start()

    rows_out(1)
    rows_out(2)

    @pl.when((even == 1) & (y > 0))
    def _():
        down.wait_recv()

    @pl.when((even == 0) & (y < 3))
    def _():
        up.wait_recv()

    rows_out(3)

    @pl.when(y > 0)
    def _():
        up.wait_send()

    @pl.when(y < 3)
    def _():
        down.wait_send()

    for p in range(2):
        for d in range(1, 8):
            forward(p, d).wait_send()
    for p in range(4):
        finish(p)


def local(tracers, courant, assignment, species_gain, w_in, b_in, w_mid, b_mid, w_out, b_out):
    f32, bf16 = jnp.float32, jnp.bfloat16
    dma = pltpu.SemaphoreType.DMA
    operands = (
        tracers, courant, assignment.reshape(1, 80), species_gain.reshape(1, 80), w_in, b_in.reshape(1, 256),
        w_mid, b_mid, w_out, b_out.reshape(1, 80),
    )
    scratch = [
        ((2, 80, 8, 128), f32), ((22, 80, 128), f32), ((2, 80, 128), f32), ((80, 128), f32), ((5, 80, 128), f32),
        ((4, 80, 8, 128), f32), ((2, 16, 128), f32), ((2, 8, 128), f32), ((8, 128), f32), ((8, 128), f32),
        ((8, 128), f32), ((2, 2, 16, 128), f32), ((2, 2, 16, 128), f32), ((16, 8, 128), f32), ((17, 8, 128), f32),
        ((2, 2, 8, 128), f32),
        ((1, 80), jnp.int32), ((1, 80), f32), ((256, 80), bf16), ((1, 256), f32), ((2, 256, 256), bf16),
        ((2, 256), f32), ((80, 256), bf16), ((1, 80), f32),
        ((256, 80), bf16), ((80, 256), bf16), ((3, 256, 128), f32), ((80, 128), f32), ((80, 128), f32),
    ]
    semaphores = [(2, 8), (2, 8), (2,), (9,), (2, 2), (2, 2), (2,), (2,), (2,), (2,), (2,), (2,), (4, 8), (4, 8), (4,)]
    return pl.pallas_call(
        kernel,
        out_shape=jax.ShapeDtypeStruct(tracers.shape, f32),
        in_specs=[pl.BlockSpec(memory_space=pl.ANY)] * len(operands),
        out_specs=pl.BlockSpec(memory_space=pl.ANY),
        scratch_shapes=[pltpu.VMEM(*s) for s in scratch] + [dma(s) for s in semaphores],
        compiler_params=pltpu.CompilerParams(
            collective_id=0, has_side_effects=True, vmem_limit_bytes=32 * 1024 * 1024
        ),
        cost_estimate=pl.CostEstimate(flops=704_000_000, bytes_accessed=4_000_000, transcendentals=1_600_000),
    )(*operands)


def solution(mesh):
    in_specs = (P("trc", None, "ty", "tx"), P(None, "trc", "ty", "tx")) + (P(),) * 8
    out_specs = P("trc", None, "ty", "tx")
    return jax.shard_map(local, mesh=mesh, in_specs=in_specs, out_specs=out_specs, check_vma=False)
```

time: 141 us -> 63.6 us (0.45)
  Pallas kernels: 0 us -> 59.4 us
  blocking collectives: 41.3 us -> 0 us
  local copies, waits for them, and re-layouts: 42 us -> 3.85 us
  waiting for transfers between devices: 23.4 us -> 0 us
  starting transfers between devices: 22.4 us -> 0 us
  other arithmetic: 8.27 us -> 0 us
  matrix products: 3.13 us -> 0 us
    pallas_call x0 -> x1, Pallas kernels: none -> 59.4 us  [local(): pl.pallas_call(kernel, out_shape=jax.ShapeDtypeStruct(tracers.shape, f32)...]
    all_gather x1 -> x0, blocking collectives: 20.7 us -> none  [local(): wind_field = lax.all_gather(courant, 'trc', axis=1, tiled=True)]
    all_to_all x1 -> x0, blocking collectives: 20.6 us -> none  [local(): lax.all_to_all(result, 'trc', split_axis=0, concat_axis=2, tiled=True)]
    unnamed x23 -> x20, local copies, waits for them, and re-layouts: 23.1 us -> 3.85 us
    ppermute x4 -> x0, starting transfers between devices: 16.9 us -> none  [the longest x2 11.7 us: extended(): after = lax.ppermute(initial, axis, down)]
    all_to_all x1 -> x0, waiting for transfers between devices: 13.3 us -> none  [local(): lax.all_to_all(by_cells, 'trc', split_axis=2, concat_axis=0, tiled=True)]
    ppermute x4 -> x0, waiting for transfers between devices: 10.2 us -> none  [the longest x2 7.49 us: extended(): after = lax.ppermute(initial, axis, down)]
    all_to_all x3 -> x0, local copies, waits for them, and re-layouts: 6.15 us -> none  [the longest x2 5.77 us: local(): lax.all_to_all(by_cells, 'trc', split_axis=2, concat_axis=0, tiled=True)]
  transfers between devices with their start and end apart: 5 -> 0, of which waited for: 5 -> 0; matrix products, arithmetic and copies ran while one was open for 4% -> 0% of each run, Pallas kernels for 0% -> 0%
where the time goes in v1:
time: 63.6 us; the launch traced here: 63.3 us
  Pallas kernels  59.4 us (93%)
  local copies, waits for them, and re-layouts  3.85 us (6%)
    pallas_call x1, Pallas kernels, local(): pl.pallas_call(kernel, out_shape=jax.ShapeDtypeStruct(tracers.shape, f32)...  59.4 us
    unnamed x20, local copies, waits for them, and re-layouts  3.85 us

profile of v1, /device:TPU:1, one launch (start us, length us, event | category | flops | bytes accessed | tf_op | source)
XLA Modules:
  0.0 63.3 jit_solution(5383094239114357692)
XLA Ops:
  0.0 0.0 copy-start.2
  0.0 0.0 copy-start.3
  0.0 0.0 copy-start.4
  0.0 0.0 copy-start.5
  0.0 0.0 copy-start.6
  0.0 0.0 copy-start.7
  0.0 0.0 copy-start.8
  0.0 1.0 %copy.11.win_ref = bf16[256,80]{1,0:T(8,128)(2,1)S(1)} copy(bf16[256,80]{0,1:T(8,128)(2,1)} %param.14) | data formatting | bytes 81920 | tf_op args[4]
  1.0 0.0 copy-done.2
  1.0 0.0 copy-done.3
  1.0 0.0 copy-done.4
  1.0 0.0 copy-done.5
  1.0 0.0 copy-done.6
  1.1 0.0 copy-done.7
  1.1 0.0 copy-done.8
  1.1 0.0 copy-start
  1.1 1.1 %copy-done = f32[10,8,16,128]{3,2,1,0:T(8,128)S(1)} copy-done((f32[10,8,16,128]{3,2,1,0:T(8,128)S(1)}, f32[10,8,16,128]{3,2,1,0:T(8,128)}, u32[]{:S(2)}) %copy-start) | copy-done | bytes 655384
  2.2 0.0 copy-start.1
  2.2 0.9 %copy-done.1 = bf16[2,256,256]{2,1,0:T(8,128)(2,1)S(1)} copy-done((bf16[2,256,256]{2,1,0:T(8,128)(2,1)S(1)}, bf16[2,256,256]{2,1,0:T(8,128)(2,1)}, u32[]{:S(2)}) %copy-start.1) | copy-done | bytes 262168
  3.1 59.4 %shard_map.100 = f32[10,8,16,128]{3,2,1,0:T(8,128)S(1)} custom-call(f32[10,8,16,128]{3,2,1,0:T(8,128)S(1)} %copy-done, f32[2,1,16,128]{3,2,1,0:T(8,128)S(1)} %copy-done.3, s32[1,80]{1,0:T(1,128)S(1)} %bitcast.5, f32[1,80]{1,0:T(1,128)S(1)} %bitcast.6, bf16[256,80]{1,0:T(8,128)(2,1)S(1)} %copy.11.win_ref, f32[1,256]{1,0:T(1,128)S(1)} %bitcast.4, ...), custom_call_target="tpu_custom_call" | custom-call | flops 704000000 | bytes 4000000 | tf_op jit(solution)/shard_map/pallas_call | solution.py:377
  62.5 0.8 %copy.13 = f32[10,8,16,128]{3,2,1,0:T(8,128)} copy(f32[10,8,16,128]{3,2,1,0:T(8,128)S(1)} %shard_map.100) | data formatting | bytes 1310720
Async XLA Ops:
  0.0 1.0 %copy-start.2 = (bf16[80,256]{1,0:T(8,128)(2,1)S(1)}, bf16[80,256]{1,0:T(8,128)(2,1)}, u32[]{:S(2)}) copy-start(bf16[80,256]{1,0:T(8,128)(2,1)} %wout_ref.1) | copy-start | bytes 122884
  0.0 1.0 %copy-start.3 = (f32[2,1,16,128]{3,2,1,0:T(8,128)S(1)}, f32[2,1,16,128]{3,2,1,0:T(8,128)}, u32[]{:S(2)}) copy-start(f32[2,1,16,128]{3,2,1,0:T(8,128)} %c_ref.1) | copy-start | bytes 49156
  0.0 1.0 %copy-start.4 = (f32[2,256]{1,0:T(2,128)S(1)}, f32[2,256]{1,0:T(2,128)}, u32[]{:S(2)}) copy-start(f32[2,256]{1,0:T(2,128)} %bmid_ref.1) | copy-start | bytes 6148
  0.0 1.0 %copy-start.5 = (f32[256]{0:T(256)S(1)}, f32[256]{0:T(256)}, u32[]{:S(2)}) copy-start(f32[256]{0:T(256)} %param.15) | copy-start | bytes 3076
  0.0 1.0 %copy-start.6 = (s32[80]{0:T(128)S(1)}, s32[80]{0:T(128)}, u32[]{:S(2)}) copy-start(s32[80]{0:T(128)} %param.12) | copy-start | bytes 964
  0.0 1.0 %copy-start.7 = (f32[80]{0:T(128)S(1)}, f32[80]{0:T(128)}, u32[]{:S(2)}) copy-start(f32[80]{0:T(128)} %param.13) | copy-start | bytes 964
  0.0 1.0 %copy-start.8 = (f32[80]{0:T(128)S(1)}, f32[80]{0:T(128)}, u32[]{:S(2)}) copy-start(f32[80]{0:T(128)} %param.19) | copy-start | bytes 964
  1.1 1.1 %copy-start = (f32[10,8,16,128]{3,2,1,0:T(8,128)S(1)}, f32[10,8,16,128]{3,2,1,0:T(8,128)}, u32[]{:S(2)}) copy-start(f32[10,8,16,128]{3,2,1,0:T(8,128)} %x_ref.1) | copy-start | bytes 1966084
  2.2 0.9 %copy-start.1 = (bf16[2,256,256]{2,1,0:T(8,128)(2,1)S(1)}, bf16[2,256,256]{2,1,0:T(8,128)(2,1)}, u32[]{:S(2)}) copy-start(bf16[2,256,256]{2,1,0:T(8,128)(2,1)} %wmid_ref.1) | copy-start | bytes 786436

commit v2 on v1

--- a/solution.py
+++ b/solution.py
@@ -8,9 +8,9 @@
 from jax.sharding import PartitionSpec as P
 
 MESH = pl.DeviceIdType.MESH
-GROUPS = (5, 4, 4, 3)
-STARTS_EVEN = (11, 7, 3, 0)
-STARTS_ODD = (0, 5, 9, 13)
+GROUPS = (2, 3, 4, 4, 3)
+STARTS_EVEN = (11, 13, 7, 3, 0)
+STARTS_ODD = (3, 0, 5, 9, 13)
 
 
 def upwind(f):
@@ -49,10 +49,10 @@
 def kernel(
     x_ref, c_ref, as_ref, gain_ref, win_ref, bin_ref, wmid_ref, bmid_ref, wout_ref, bout_ref,
     o_ref,
-    got, swept, strip, fixed, adv, back, cv, c1h, eco, ecl, ecr, t_out, t_in, cc, cf, sc,
+    xv, got, swept, strip, fixed, adv, back, cv, c1h, eco, ecl, ecr, q_out, q_in, cc, cf, sc,
     v_as, v_gain, v_win, v_bin, v_wmid, v_bmid, v_wout, v_bout,
     first_w, last_w, bias_b, last_b, gain_b,
-    fs, fr, fl, lw, ts, tr, es, er, c1s, c1r, hs, hr, os_, or_, ol,
+    fs, fr, fl, lw, qs, qr, ready, es, er, c1s, c1r, hs, hr, os_, or_, ol,
 ):
     me, y, x = lax.axis_index("trc"), lax.axis_index("ty"), lax.axis_index("tx")
     even = 1 - lax.rem(y, 2)
@@ -67,7 +67,7 @@
     loads = [
         pltpu.make_async_copy(src, dst, lw.at[i])
         for i, (src, dst) in enumerate((
-            (c_ref.at[:, 0], cv), (as_ref, v_as), (gain_ref, v_gain), (win_ref, v_win), (bin_ref, v_bin),
+            (c_ref.at[:, 0], cv), (x_ref, xv), (as_ref, v_as), (gain_ref, v_gain), (win_ref, v_win), (bin_ref, v_bin),
             (wmid_ref, v_wmid), (bmid_ref, v_bmid), (wout_ref, v_wout), (bout_ref, v_bout),
         ))
     ]
@@ -78,8 +78,16 @@
     barrier = pltpu.get_barrier_semaphore()
     for d in range(1, 8):
         pl.semaphore_signal(barrier, inc=1, device_id={"trc": peer(d)}, device_id_type=MESH)
-    for to in (left, right, {"ty": lax.rem(y + 3, 4)}, {"ty": lax.rem(y + 1, 4)}):
-        pl.semaphore_signal(barrier, inc=1, device_id=to, device_id_type=MESH)
+    for d in (1, 3):
+        pl.semaphore_signal(barrier, inc=1, device_id={"ty": lax.rem(y + d, 4)}, device_id_type=MESH)
+
+    first = lax.rem(x, 2) == 0
+
+    @pl.when(first)
+    def _():
+        for side in (left, right):
+            for k in range(8):
+                pl.semaphore_signal(barrier, inc=1, device_id={"trc": k, **side}, device_id_type=MESH)
 
     lane8 = lax.broadcasted_iota(jnp.int32, (8, 128), 1)
     lane16 = lax.broadcasted_iota(jnp.int32, (16, 128), 1)
@@ -102,11 +110,49 @@
     def _():
         swept[19:22] = jnp.zeros((3, 80, 128), jnp.float32)
 
-    pl.semaphore_wait(barrier, 11)
+    loads[1].wait()
+    xv2 = xv.reshape(1280, 128)
+    at16 = lane8 % 16
+
+    @pl.loop(0, 10)
+    def _(g):
+        part = [jnp.zeros((8, 128), jnp.float32)] * 2
+        for h in range(2):
+            for i in range(8):
+                v = pltpu.roll(xv2[pl.ds(g * 128 + 8 * h + i, 8, stride=16), :], (16 * i + 8) % 128, 1)
+                part[h] = jnp.where(lane8 // 16 == i, v, part[h])
+        q = jnp.where(at16 < 8, pltpu.roll(part[1], 125, 1), pltpu.roll(part[1], 3, 1))
+        q_out[pl.ds(pl.multiple_of(g * 8, 8), 8), :] = jnp.where((at16 >= 5) & (at16 <= 10), part[0], q)
+
+    q_out3 = q_out.reshape(10, 8, 128)
+
+    def edges(side, k):
+        return remote(
+            q_out3.at[:, k], q_in.at[1 - side, pl.ds(10 * me, 10)], qs.at[side, k], qr.at[1 - side, me],
+            {"trc": k, **(left, right)[side]},
+        )
 
     ec_copies = (remote(eco, ecr, es.at[0], er.at[0], left), remote(eco, ecl, es.at[1], er.at[1], right))
-    for copy in ec_copies:
-        copy.start()
+
+    def send_edges():
+        for copy in ec_copies:
+            copy.start()
+        for side in range(2):
+            for k in range(8):
+                edges(side, k).start()
+
+    @pl.when(first)
+    def _():
+        pl.semaphore_wait(barrier, 9)
+
+    @pl.when(jnp.logical_not(first))
+    def _():
+        pl.semaphore_wait(barrier, 25)
+        for side in (left, right):
+            for k in range(8):
+                pl.semaphore_signal(ready, inc=1, device_id={"trc": k, **side}, device_id_type=MESH)
+        send_edges()
+
     wind_up = remote(cv.at[1, pl.ds(0, 1)], c1h.at[1, pl.ds(0, 1)], c1s.at[0], c1r.at[0], {"ty": y - 1})
     wind_down = remote(cv.at[1, pl.ds(15, 1)], c1h.at[0, pl.ds(0, 1)], c1s.at[1], c1r.at[1], {"ty": y + 1})
 
@@ -141,7 +187,7 @@
             forward(p, d).start()
         own(p).start()
 
-    for load in loads[1:]:
+    for load in loads[2:]:
         load.wait()
     species = lax.broadcasted_iota(jnp.int32, (80, 80), 1)
     held = column_of(v_as[...].astype(jnp.float32), 80).astype(jnp.int32)
@@ -163,16 +209,28 @@
     for i in range(6):
         cc[:, i, :] = coef[i]
 
-    for copy in ec_copies:
-        copy.wait()
+    @pl.when(first)
+    def _():
+        pl.semaphore_wait(ready, 16)
+        send_edges()
+
     inner = lane8 % 16 < 8
-    for side, wind8 in enumerate((jnp.where(inner, ecl[...], eco[...]), jnp.where(inner, eco[...], ecr[...]))):
-        at_left = 0.5 * (pltpu.roll(wind8, 1, 1) + wind8)
-        at_right = pltpu.roll(at_left, 127, 1)
-        coef = upwind(at_right)[:3] + upwind(at_left)[3:]
-        for i in range(6):
-            sc[side, 0, i : i + 1, :] = coef[i][0:1]
-            sc[side, 1, i : i + 1, :] = coef[i][1:2]
+
+    def strip_coefficients():
+        for copy in ec_copies:
+            copy.wait()
+        for side in range(2):
+            for k in range(8):
+                there = q_in.at[1 - side, pl.ds(10 * k, 10)]
+                remote(q_out3.at[:, k], there, qs.at[side, k], qr.at[1 - side, k], {"trc": k, **(left, right)[side]}).wait()
+        winds = (jnp.where(inner, ecl[...], eco[...]), jnp.where(inner, eco[...], ecr[...]))
+        for side, wind8 in enumerate(winds):
+            at_left = 0.5 * (pltpu.roll(wind8, 1, 1) + wind8)
+            at_right = pltpu.roll(at_left, 127, 1)
+            coef = upwind(at_right)[:3] + upwind(at_left)[3:]
+            for i in range(6):
+                sc[side, 0, i : i + 1, :] = coef[i][0:1]
+                sc[side, 1, i : i + 1, :] = coef[i][1:2]
 
     @pl.when(y > 0)
     def _():
@@ -194,7 +252,7 @@
         cf[16, i : i + 1, :] = coef[i]
 
     got2 = [got.at[p].reshape(640, 128) for p in range(2)]
-    back2 = [back.at[p].reshape(640, 128) for p in range(4)]
+    back2 = [back.at[p].reshape(640, 128) for p in range(5)]
 
     def row_coef(ref, *at):
         return [ref[(*at, pl.ds(i, 1), slice(None))] for i in range(6)]
@@ -213,18 +271,6 @@
                 e = jnp.where(lane8 // 16 == i, pltpu.roll(q, (16 * i + 8) % 128, 1), e)
             strip[p, pl.ds(pl.multiple_of(g * 8, 8), 8), :] = e
 
-        for side, first in enumerate((8, 5)):
-            for u in range(2):
-                t = None
-                for slot in range(5):
-                    e = pltpu.roll(strip[p, 16 * slot + 8 * u : 16 * slot + 8 * u + 8, :], (3 * slot - first) % 128, 1)
-                    t = e if t is None else jnp.where((lane8 % 16) // 3 == slot, e, t)
-                t_out[p, side, 8 * u : 8 * u + 8, :] = t
-        to_left = remote(t_out.at[p, 0], t_in.at[p, 1], ts.at[p, 0], tr.at[p, 1], left)
-        to_right = remote(t_out.at[p, 1], t_in.at[p, 0], ts.at[p, 1], tr.at[p, 0], right)
-        to_left.start()
-        to_right.start()
-
         @pl.loop(0, 8)
         def _(i):
             coef = row_coef(cc, base + i)
@@ -232,14 +278,14 @@
                 q = got2[p][pl.ds(g * 8 + i, 16, stride=8), :]
                 swept[base + i + 3, g : g + 16, :] = sweep_lanes(q, coef)
 
-        to_left.wait()
-        to_right.wait()
+        if p == 0:
+            strip_coefficients()
         coefs = [row_coef(sc, side, base // 8) for side in range(2)]
+        h = base // 8
         for g in range(10):
-            slot, u = g // 2, g % 2
             mine = strip[p, 8 * g : 8 * g + 8, :]
-            before = pltpu.roll(t_in[p, 0, 8 * u : 8 * u + 8, :], (5 - 3 * slot) % 128, 1)
-            after = pltpu.roll(t_in[p, 1, 8 * u : 8 * u + 8, :], (8 - 3 * slot) % 128, 1)
+            before = pltpu.roll(q_in[0, 8 * g : 8 * g + 8, :], 3 * h, 1)
+            after = pltpu.roll(q_in[1, 8 * g : 8 * g + 8, :], lax.rem(128 - 3 * h, 128), 1)
             new_left = sweep_lanes(jnp.where(inner, before, mine), coefs[0])
             new_right = sweep_lanes(jnp.where(inner, mine, after), coefs[1])
             fixed[8 * g : 8 * g + 8, :] = jnp.where(inner, new_right, new_left)
@@ -310,6 +356,8 @@
     def _():
         up.start()
 
+    rows_out(0)
+
     @pl.when(even == 1)
     def _():
         up.wait_recv()
@@ -318,7 +366,7 @@
     def _():
         down.wait_recv()
 
-    rows_out(0)
+    rows_out(1)
     half(1)
 
     @pl.when((even == 1) & (y > 0))
@@ -329,8 +377,8 @@
     def _():
         down.start()
 
-    rows_out(1)
     rows_out(2)
+    rows_out(3)
 
     @pl.when((even == 1) & (y > 0))
     def _():
@@ -340,7 +388,7 @@
     def _():
         up.wait_recv()
 
-    rows_out(3)
+    rows_out(4)
 
     @pl.when(y > 0)
     def _():
@@ -353,7 +401,7 @@
     for p in range(2):
         for d in range(1, 8):
             forward(p, d).wait_send()
-    for p in range(4):
+    for p in range(5):
         finish(p)
 
 
@@ -365,21 +413,24 @@
         w_mid, b_mid, w_out, b_out.reshape(1, 80),
     )
     scratch = [
-        ((2, 80, 8, 128), f32), ((22, 80, 128), f32), ((2, 80, 128), f32), ((80, 128), f32), ((5, 80, 128), f32),
-        ((4, 80, 8, 128), f32), ((2, 16, 128), f32), ((2, 8, 128), f32), ((8, 128), f32), ((8, 128), f32),
-        ((8, 128), f32), ((2, 2, 16, 128), f32), ((2, 2, 16, 128), f32), ((16, 8, 128), f32), ((17, 8, 128), f32),
+        ((10, 8, 16, 128), f32), ((2, 80, 8, 128), f32), ((22, 80, 128), f32), ((2, 80, 128), f32), ((80, 128), f32), ((5, 80, 128), f32),
+        ((5, 80, 8, 128), f32), ((2, 16, 128), f32), ((2, 8, 128), f32), ((8, 128), f32), ((8, 128), f32),
+        ((8, 128), f32), ((80, 128), f32), ((2, 80, 128), f32), ((16, 8, 128), f32), ((17, 8, 128), f32),
         ((2, 2, 8, 128), f32),
         ((1, 80), jnp.int32), ((1, 80), f32), ((256, 80), bf16), ((1, 256), f32), ((2, 256, 256), bf16),
         ((2, 256), f32), ((80, 256), bf16), ((1, 80), f32),
         ((256, 80), bf16), ((80, 256), bf16), ((3, 256, 128), f32), ((80, 128), f32), ((80, 128), f32),
     ]
-    semaphores = [(2, 8), (2, 8), (2,), (9,), (2, 2), (2, 2), (2,), (2,), (2,), (2,), (2,), (2,), (4, 8), (4, 8), (4,)]
+    semaphores = [
+        dma((2, 8)), dma((2, 8)), dma((2,)), dma((10,)), dma((2, 8)), dma((2, 8)), pltpu.SemaphoreType.REGULAR,
+        dma((2,)), dma((2,)), dma((2,)), dma((2,)), dma((2,)), dma((2,)), dma((5, 8)), dma((5, 8)), dma((5,)),
+    ]
     return pl.pallas_call(
         kernel,
         out_shape=jax.ShapeDtypeStruct(tracers.shape, f32),
         in_specs=[pl.BlockSpec(memory_space=pl.ANY)] * len(operands),
         out_specs=pl.BlockSpec(memory_space=pl.ANY),
-        scratch_shapes=[pltpu.VMEM(*s) for s in scratch] + [dma(s) for s in semaphores],
+        scratch_shapes=[pltpu.VMEM(*s) for s in scratch] + semaphores,
         compiler_params=pltpu.CompilerParams(
             collective_id=0, has_side_effects=True, vmem_limit_bytes=32 * 1024 * 1024
         ),

time: 63.6 us -> 52.6 us (0.83); the launches traced: 63.3 us -> 51.5 us
  Pallas kernels: 59.4 us -> 47.6 us
    pallas_call x1, Pallas kernels: 59.4 us -> 47.6 us  [local(): pl.pallas_call(kernel, out_shape=jax.ShapeDtypeStruct(tracers.shape, f32)...]
where the time goes in v2:
time: 52.6 us; the launch traced here: 51.5 us
  Pallas kernels  47.6 us (90%)
  local copies, waits for them, and re-layouts  3.85 us (7%)
    pallas_call x1, Pallas kernels, local(): pl.pallas_call(kernel, out_shape=jax.ShapeDtypeStruct(tracers.shape, f32)...  47.6 us
    unnamed x20, local copies, waits for them, and re-layouts  3.85 us

profile of v2, /device:TPU:1, one launch (start us, length us, event | category | flops | bytes accessed | tf_op | source)
XLA Modules:
  0.0 51.5 jit_solution(4057603121784486514)
XLA Ops:
  0.0 0.0 copy-start.2
  0.0 0.0 copy-start.3
  0.0 0.0 copy-start.4
  0.0 0.0 copy-start.5
  0.0 0.0 copy-start.6
  0.0 0.0 copy-start.7
  0.0 0.0 copy-start.8
  0.0 1.0 %copy.11.win_ref = bf16[256,80]{1,0:T(8,128)(2,1)S(1)} copy(bf16[256,80]{0,1:T(8,128)(2,1)} %param.14) | data formatting | bytes 81920 | tf_op args[4]
  1.0 0.0 copy-done.2
  1.0 0.0 copy-done.3
  1.0 0.0 copy-done.4
  1.0 0.0 copy-done.5
  1.0 0.0 copy-done.6
  1.1 0.0 copy-done.7
  1.1 0.0 copy-done.8
  1.1 0.0 copy-start
  1.1 1.1 %copy-done = f32[10,8,16,128]{3,2,1,0:T(8,128)S(1)} copy-done((f32[10,8,16,128]{3,2,1,0:T(8,128)S(1)}, f32[10,8,16,128]{3,2,1,0:T(8,128)}, u32[]{:S(2)}) %copy-start) | copy-done | bytes 655384
  2.2 0.0 copy-start.1
  2.2 0.9 %copy-done.1 = bf16[2,256,256]{2,1,0:T(8,128)(2,1)S(1)} copy-done((bf16[2,256,256]{2,1,0:T(8,128)(2,1)S(1)}, bf16[2,256,256]{2,1,0:T(8,128)(2,1)}, u32[]{:S(2)}) %copy-start.1) | copy-done | bytes 262168
  3.1 47.6 %shard_map.100 = f32[10,8,16,128]{3,2,1,0:T(8,128)S(1)} custom-call(f32[10,8,16,128]{3,2,1,0:T(8,128)S(1)} %copy-done, f32[2,1,16,128]{3,2,1,0:T(8,128)S(1)} %copy-done.3, s32[1,80]{1,0:T(1,128)S(1)} %bitcast.5, f32[1,80]{1,0:T(1,128)S(1)} %bitcast.6, bf16[256,80]{1,0:T(8,128)(2,1)S(1)} %copy.11.win_ref, f32[1,256]{1,0:T(1,128)S(1)} %bitcast.4, ...), custom_call_target="tpu_custom_call" | custom-call | flops 704000000 | bytes 4000000 | tf_op jit(solution)/shard_map/pallas_call | solution.py:428
  50.7 0.8 %copy.13 = f32[10,8,16,128]{3,2,1,0:T(8,128)} copy(f32[10,8,16,128]{3,2,1,0:T(8,128)S(1)} %shard_map.100) | data formatting | bytes 1310720
Async XLA Ops:
  0.0 1.0 %copy-start.2 = (bf16[80,256]{1,0:T(8,128)(2,1)S(1)}, bf16[80,256]{1,0:T(8,128)(2,1)}, u32[]{:S(2)}) copy-start(bf16[80,256]{1,0:T(8,128)(2,1)} %wout_ref.1) | copy-start | bytes 122884
  0.0 1.0 %copy-start.3 = (f32[2,1,16,128]{3,2,1,0:T(8,128)S(1)}, f32[2,1,16,128]{3,2,1,0:T(8,128)}, u32[]{:S(2)}) copy-start(f32[2,1,16,128]{3,2,1,0:T(8,128)} %c_ref.1) | copy-start | bytes 49156
  0.0 1.0 %copy-start.4 = (f32[2,256]{1,0:T(2,128)S(1)}, f32[2,256]{1,0:T(2,128)}, u32[]{:S(2)}) copy-start(f32[2,256]{1,0:T(2,128)} %bmid_ref.1) | copy-start | bytes 6148
  0.0 1.0 %copy-start.5 = (f32[256]{0:T(256)S(1)}, f32[256]{0:T(256)}, u32[]{:S(2)}) copy-start(f32[256]{0:T(256)} %param.15) | copy-start | bytes 3076
  0.0 1.0 %copy-start.6 = (s32[80]{0:T(128)S(1)}, s32[80]{0:T(128)}, u32[]{:S(2)}) copy-start(s32[80]{0:T(128)} %param.12) | copy-start | bytes 964
  0.0 1.0 %copy-start.7 = (f32[80]{0:T(128)S(1)}, f32[80]{0:T(128)}, u32[]{:S(2)}) copy-start(f32[80]{0:T(128)} %param.13) | copy-start | bytes 964
  0.0 1.0 %copy-start.8 = (f32[80]{0:T(128)S(1)}, f32[80]{0:T(128)}, u32[]{:S(2)}) copy-start(f32[80]{0:T(128)} %param.19) | copy-start | bytes 964
  1.1 1.1 %copy-start = (f32[10,8,16,128]{3,2,1,0:T(8,128)S(1)}, f32[10,8,16,128]{3,2,1,0:T(8,128)}, u32[]{:S(2)}) copy-start(f32[10,8,16,128]{3,2,1,0:T(8,128)} %x_ref.1) | copy-start | bytes 1966084
  2.2 0.9 %copy-start.1 = (bf16[2,256,256]{2,1,0:T(8,128)(2,1)S(1)}, bf16[2,256,256]{2,1,0:T(8,128)(2,1)}, u32[]{:S(2)}) copy-start(bf16[2,256,256]{2,1,0:T(8,128)(2,1)} %wmid_ref.1) | copy-start | bytes 786436

commit v3 on v2

--- a/solution.py
+++ b/solution.py
@@ -110,11 +110,29 @@
     def _():
         swept[19:22] = jnp.zeros((3, 80, 128), jnp.float32)
 
+    halves = (8 * even, 8 * (1 - even))
+
+    def forward(p, d):
+        k = peer(d)
+        rows = pl.ds(pl.multiple_of(halves[p], 8), 8)
+        return remote(
+            x_ref.at[:, k, rows], got.at[p, pl.ds(10 * me, 10)], fs.at[p, k], fr.at[p, me], {"trc": k}
+        )
+
+    def arriving(p, d):
+        k = peer(d)
+        there = got.at[p, pl.ds(10 * k, 10)]
+        return remote(there, there, fs.at[p, k], fr.at[p, k], {"trc": k})
+
+    def own(p):
+        rows = pl.ds(pl.multiple_of(halves[p], 8), 8)
+        return pltpu.make_async_copy(x_ref.at[:, me, rows], got.at[p, pl.ds(10 * me, 10)], fl.at[p])
+
     loads[1].wait()
     xv2 = xv.reshape(1280, 128)
     at16 = lane8 % 16
 
-    @pl.loop(0, 10)
+    @pl.loop(0, 10, unroll=5)
     def _(g):
         part = [jnp.zeros((8, 128), jnp.float32)] * 2
         for h in range(2):
@@ -134,58 +152,54 @@
 
     ec_copies = (remote(eco, ecr, es.at[0], er.at[0], left), remote(eco, ecl, es.at[1], er.at[1], right))
 
-    def send_edges():
-        for copy in ec_copies:
-            copy.start()
-        for side in range(2):
-            for k in range(8):
-                edges(side, k).start()
-
-    @pl.when(first)
-    def _():
-        pl.semaphore_wait(barrier, 9)
-
-    @pl.when(jnp.logical_not(first))
-    def _():
-        pl.semaphore_wait(barrier, 25)
-        for side in (left, right):
-            for k in range(8):
-                pl.semaphore_signal(ready, inc=1, device_id={"trc": k, **side}, device_id_type=MESH)
-        send_edges()
-
-    wind_up = remote(cv.at[1, pl.ds(0, 1)], c1h.at[1, pl.ds(0, 1)], c1s.at[0], c1r.at[0], {"ty": y - 1})
-    wind_down = remote(cv.at[1, pl.ds(15, 1)], c1h.at[0, pl.ds(0, 1)], c1s.at[1], c1r.at[1], {"ty": y + 1})
-
-    @pl.when(y > 0)
-    def _():
-        wind_up.start()
-
-    @pl.when(y < 3)
-    def _():
-        wind_down.start()
-
-    halves = (8 * even, 8 * (1 - even))
-
-    def forward(p, d):
-        k = peer(d)
-        rows = pl.ds(pl.multiple_of(halves[p], 8), 8)
-        return remote(
-            x_ref.at[:, k, rows], got.at[p, pl.ds(10 * me, 10)], fs.at[p, k], fr.at[p, me], {"trc": k}
-        )
-
-    def arriving(p, d):
-        k = peer(d)
-        there = got.at[p, pl.ds(10 * k, 10)]
-        return remote(there, there, fs.at[p, k], fr.at[p, k], {"trc": k})
-
-    def own(p):
-        rows = pl.ds(pl.multiple_of(halves[p], 8), 8)
-        return pltpu.make_async_copy(x_ref.at[:, me, rows], got.at[p, pl.ds(10 * me, 10)], fl.at[p])
-
-    for p in range(2):
+    def send_edges(side):
+        ec_copies[side].start()
+        for k in range(8):
+            edges(side, k).start()
+
+    def send_half(p):
         for d in range(1, 8):
             forward(p, d).start()
         own(p).start()
+
+    def greeted(side):
+        pl.semaphore_wait(ready.at[side], 8)
+
+    @pl.when(first)
+    def _():
+        pl.semaphore_wait(barrier, 9)
+        send_half(0)
+        greeted(1)
+        send_edges(1)
+
+        @pl.when(x > 0)
+        def _():
+            greeted(0)
+            send_edges(0)
+
+        send_half(1)
+
+    @pl.when(jnp.logical_not(first))
+    def _():
+        pl.semaphore_wait(barrier, 25)
+        send_edges(1)
+        for side, to in enumerate((left, right)):
+            for k in range(8):
+                pl.semaphore_signal(ready.at[1 - side], inc=1, device_id={"trc": k, **to}, device_id_type=MESH)
+        send_edges(0)
+        send_half(0)
+        send_half(1)
+
+    wind_up = remote(cv.at[1, pl.ds(0, 1)], c1h.at[1, pl.ds(0, 1)], c1s.at[0], c1r.at[0], {"ty": y - 1})
+    wind_down = remote(cv.at[1, pl.ds(15, 1)], c1h.at[0, pl.ds(0, 1)], c1s.at[1], c1r.at[1], {"ty": y + 1})
+
+    @pl.when(y > 0)
+    def _():
+        wind_up.start()
+
+    @pl.when(y < 3)
+    def _():
+        wind_down.start()
 
     for load in loads[2:]:
         load.wait()
@@ -209,20 +223,20 @@
     for i in range(6):
         cc[:, i, :] = coef[i]
 
-    @pl.when(first)
-    def _():
-        pl.semaphore_wait(ready, 16)
-        send_edges()
+    @pl.when(x == 0)
+    def _():
+        greeted(0)
+        send_edges(0)
 
     inner = lane8 % 16 < 8
 
     def strip_coefficients():
         for copy in ec_copies:
-            copy.wait()
+            copy.wait_recv()
         for side in range(2):
             for k in range(8):
-                there = q_in.at[1 - side, pl.ds(10 * k, 10)]
-                remote(q_out3.at[:, k], there, qs.at[side, k], qr.at[1 - side, k], {"trc": k, **(left, right)[side]}).wait()
+                there = q_in.at[side, pl.ds(10 * k, 10)]
+                remote(there, there, qs.at[side, k], qr.at[side, k], {"trc": k, **(left, right)[side]}).wait_recv()
         winds = (jnp.where(inner, ecl[...], eco[...]), jnp.where(inner, eco[...], ecr[...]))
         for side, wind8 in enumerate(winds):
             at_left = 0.5 * (pltpu.roll(wind8, 1, 1) + wind8)
@@ -263,7 +277,7 @@
             arriving(p, d).wait_recv()
         own(p).wait()
 
-        @pl.loop(0, 10)
+        @pl.loop(0, 10, unroll=5)
         def _(g):
             e = jnp.zeros((8, 128), jnp.float32)
             for i in range(8):
@@ -271,7 +285,7 @@
                 e = jnp.where(lane8 // 16 == i, pltpu.roll(q, (16 * i + 8) % 128, 1), e)
             strip[p, pl.ds(pl.multiple_of(g * 8, 8), 8), :] = e
 
-        @pl.loop(0, 8)
+        @pl.loop(0, 8, unroll=2)
         def _(i):
             coef = row_coef(cc, base + i)
             for g in range(0, 80, 16):
@@ -398,6 +412,10 @@
     def _():
         down.wait_send()
 
+    for side in range(2):
+        ec_copies[side].wait_send()
+        for k in range(8):
+            edges(side, k).wait_send()
     for p in range(2):
         for d in range(1, 8):
             forward(p, d).wait_send()
@@ -422,7 +440,7 @@
         ((256, 80), bf16), ((80, 256), bf16), ((3, 256, 128), f32), ((80, 128), f32), ((80, 128), f32),
     ]
     semaphores = [
-        dma((2, 8)), dma((2, 8)), dma((2,)), dma((10,)), dma((2, 8)), dma((2, 8)), pltpu.SemaphoreType.REGULAR,
+        dma((2, 8)), dma((2, 8)), dma((2,)), dma((10,)), dma((2, 8)), dma((2, 8)), pltpu.SemaphoreType.REGULAR((2,)),
         dma((2,)), dma((2,)), dma((2,)), dma((2,)), dma((2,)), dma((2,)), dma((5, 8)), dma((5, 8)), dma((5,)),
     ]
     return pl.pallas_call(

time: 52.6 us -> 49.3 us (0.937); the launches traced: 51.5 us -> 49 us
  Pallas kernels: 47.6 us -> 45 us
    pallas_call x1, Pallas kernels: 47.6 us -> 45 us  [local(): pl.pallas_call(kernel, out_shape=jax.ShapeDtypeStruct(tracers.shape, f32)...]
where the time goes in v3:
time: 49.3 us; the launch traced here: 49 us
  Pallas kernels  45 us (91%)
  local copies, waits for them, and re-layouts  3.85 us (8%)
    pallas_call x1, Pallas kernels, local(): pl.pallas_call(kernel, out_shape=jax.ShapeDtypeStruct(tracers.shape, f32)...  45 us
    unnamed x20, local copies, waits for them, and re-layouts  3.85 us

profile of v3, /device:TPU:1, one launch (start us, length us, event | category | flops | bytes accessed | tf_op | source)
XLA Modules:
  0.0 49.0 jit_solution(569449431771273719)
XLA Ops:
  0.0 0.0 copy-start.2
  0.0 0.0 copy-start.3
  0.0 0.0 copy-start.4
  0.0 0.0 copy-start.5
  0.0 0.0 copy-start.6
  0.0 0.0 copy-start.7
  0.0 0.0 copy-start.8
  0.0 1.0 %copy.11.win_ref = bf16[256,80]{1,0:T(8,128)(2,1)S(1)} copy(bf16[256,80]{0,1:T(8,128)(2,1)} %param.14) | data formatting | bytes 81920 | tf_op args[4]
  1.0 0.0 copy-done.2
  1.0 0.0 copy-done.3
  1.0 0.0 copy-done.4
  1.0 0.0 copy-done.5
  1.0 0.0 copy-done.6
  1.1 0.0 copy-done.7
  1.1 0.0 copy-done.8
  1.1 0.0 copy-start
  1.1 1.1 %copy-done = f32[10,8,16,128]{3,2,1,0:T(8,128)S(1)} copy-done((f32[10,8,16,128]{3,2,1,0:T(8,128)S(1)}, f32[10,8,16,128]{3,2,1,0:T(8,128)}, u32[]{:S(2)}) %copy-start) | copy-done | bytes 655384
  2.2 0.0 copy-start.1
  2.2 0.9 %copy-done.1 = bf16[2,256,256]{2,1,0:T(8,128)(2,1)S(1)} copy-done((bf16[2,256,256]{2,1,0:T(8,128)(2,1)S(1)}, bf16[2,256,256]{2,1,0:T(8,128)(2,1)}, u32[]{:S(2)}) %copy-start.1) | copy-done | bytes 262168
  3.1 45.0 %shard_map.100 = f32[10,8,16,128]{3,2,1,0:T(8,128)S(1)} custom-call(f32[10,8,16,128]{3,2,1,0:T(8,128)S(1)} %copy-done, f32[2,1,16,128]{3,2,1,0:T(8,128)S(1)} %copy-done.3, s32[1,80]{1,0:T(1,128)S(1)} %bitcast.5, f32[1,80]{1,0:T(1,128)S(1)} %bitcast.6, bf16[256,80]{1,0:T(8,128)(2,1)S(1)} %copy.11.win_ref, f32[1,256]{1,0:T(1,128)S(1)} %bitcast.4, ...), custom_call_target="tpu_custom_call" | custom-call | flops 704000000 | bytes 4000000 | tf_op jit(solution)/shard_map/pallas_call | solution.py:446
  48.2 0.8 %copy.13 = f32[10,8,16,128]{3,2,1,0:T(8,128)} copy(f32[10,8,16,128]{3,2,1,0:T(8,128)S(1)} %shard_map.100) | data formatting | bytes 1310720
Async XLA Ops:
  0.0 1.0 %copy-start.2 = (bf16[80,256]{1,0:T(8,128)(2,1)S(1)}, bf16[80,256]{1,0:T(8,128)(2,1)}, u32[]{:S(2)}) copy-start(bf16[80,256]{1,0:T(8,128)(2,1)} %wout_ref.1) | copy-start | bytes 122884
  0.0 1.0 %copy-start.3 = (f32[2,1,16,128]{3,2,1,0:T(8,128)S(1)}, f32[2,1,16,128]{3,2,1,0:T(8,128)}, u32[]{:S(2)}) copy-start(f32[2,1,16,128]{3,2,1,0:T(8,128)} %c_ref.1) | copy-start | bytes 49156
  0.0 1.0 %copy-start.4 = (f32[2,256]{1,0:T(2,128)S(1)}, f32[2,256]{1,0:T(2,128)}, u32[]{:S(2)}) copy-start(f32[2,256]{1,0:T(2,128)} %bmid_ref.1) | copy-start | bytes 6148
  0.0 1.0 %copy-start.5 = (f32[256]{0:T(256)S(1)}, f32[256]{0:T(256)}, u32[]{:S(2)}) copy-start(f32[256]{0:T(256)} %param.15) | copy-start | bytes 3076
  0.0 1.0 %copy-start.6 = (s32[80]{0:T(128)S(1)}, s32[80]{0:T(128)}, u32[]{:S(2)}) copy-start(s32[80]{0:T(128)} %param.12) | copy-start | bytes 964
  0.0 1.0 %copy-start.7 = (f32[80]{0:T(128)S(1)}, f32[80]{0:T(128)}, u32[]{:S(2)}) copy-start(f32[80]{0:T(128)} %param.13) | copy-start | bytes 964
  0.0 1.0 %copy-start.8 = (f32[80]{0:T(128)S(1)}, f32[80]{0:T(128)}, u32[]{:S(2)}) copy-start(f32[80]{0:T(128)} %param.19) | copy-start | bytes 964
  1.1 1.1 %copy-start = (f32[10,8,16,128]{3,2,1,0:T(8,128)S(1)}, f32[10,8,16,128]{3,2,1,0:T(8,128)}, u32[]{:S(2)}) copy-start(f32[10,8,16,128]{3,2,1,0:T(8,128)} %x_ref.1) | copy-start | bytes 1966084
  2.2 0.9 %copy-start.1 = (bf16[2,256,256]{2,1,0:T(8,128)(2,1)S(1)}, bf16[2,256,256]{2,1,0:T(8,128)(2,1)}, u32[]{:S(2)}) copy-start(bf16[2,256,256]{2,1,0:T(8,128)(2,1)} %wmid_ref.1) | copy-start | bytes 786436

commit v4 on v3

--- a/solution.py
+++ b/solution.py
@@ -8,6 +8,7 @@
 from jax.sharding import PartitionSpec as P
 
 MESH = pl.DeviceIdType.MESH
+VM = 60 * 1024 * 1024
 GROUPS = (2, 3, 4, 4, 3)
 STARTS_EVEN = (11, 13, 7, 3, 0)
 STARTS_ODD = (3, 0, 5, 9, 13)
@@ -182,10 +183,10 @@
     @pl.when(jnp.logical_not(first))
     def _():
         pl.semaphore_wait(barrier, 25)
-        send_edges(1)
         for side, to in enumerate((left, right)):
             for k in range(8):
                 pl.semaphore_signal(ready.at[1 - side], inc=1, device_id={"trc": k, **to}, device_id_type=MESH)
+        send_edges(1)
         send_edges(0)
         send_half(0)
         send_half(1)
@@ -208,7 +209,7 @@
     chosen = held == species
     pick = jnp.where(chosen, 1.0, 0.0).astype(jnp.bfloat16)
     first_w[...] = lax.dot_general(
-        v_win[...], pick, (((1,), (1,)), ((), ())), preferred_element_type=jnp.float32
+        v_win[...], pick, (((0,), (1,)), ((), ())), preferred_element_type=jnp.float32
     ).astype(jnp.bfloat16)
     last_w[...] = jnp.dot(pick, v_wout[...], preferred_element_type=jnp.float32).astype(jnp.bfloat16)
     gain_b[...] = jnp.broadcast_to(jnp.sum(jnp.where(chosen, v_gain[...], 0.0), axis=1, keepdims=True), (80, 128))
@@ -427,7 +428,7 @@
     f32, bf16 = jnp.float32, jnp.bfloat16
     dma = pltpu.SemaphoreType.DMA
     operands = (
-        tracers, courant, assignment.reshape(1, 80), species_gain.reshape(1, 80), w_in, b_in.reshape(1, 256),
+        tracers, courant, assignment.reshape(1, 80), species_gain.reshape(1, 80), w_in.T, b_in.reshape(1, 256),
         w_mid, b_mid, w_out, b_out.reshape(1, 80),
     )
     scratch = [
@@ -435,7 +436,7 @@
         ((5, 80, 8, 128), f32), ((2, 16, 128), f32), ((2, 8, 128), f32), ((8, 128), f32), ((8, 128), f32),
         ((8, 128), f32), ((80, 128), f32), ((2, 80, 128), f32), ((16, 8, 128), f32), ((17, 8, 128), f32),
         ((2, 2, 8, 128), f32),
-        ((1, 80), jnp.int32), ((1, 80), f32), ((256, 80), bf16), ((1, 256), f32), ((2, 256, 256), bf16),
+        ((1, 80), jnp.int32), ((1, 80), f32), ((80, 256), bf16), ((1, 256), f32), ((2, 256, 256), bf16),
         ((2, 256), f32), ((80, 256), bf16), ((1, 80), f32),
         ((256, 80), bf16), ((80, 256), bf16), ((3, 256, 128), f32), ((80, 128), f32), ((80, 128), f32),
     ]
@@ -450,7 +451,7 @@
         out_specs=pl.BlockSpec(memory_space=pl.ANY),
         scratch_shapes=[pltpu.VMEM(*s) for s in scratch] + semaphores,
         compiler_params=pltpu.CompilerParams(
-            collective_id=0, has_side_effects=True, vmem_limit_bytes=32 * 1024 * 1024
+            collective_id=0, has_side_effects=True, vmem_limit_bytes=VM
         ),
         cost_estimate=pl.CostEstimate(flops=704_000_000, bytes_accessed=4_000_000, transcendentals=1_600_000),
     )(*operands)

time: 49.3 us -> 46.9 us (0.951)
  local copies, waits for them, and re-layouts: 3.85 us -> 1.97 us
    unnamed x20 -> x1, local copies, waits for them, and re-layouts: 3.85 us -> 1.97 us
where the time goes in v4:
time: 46.9 us; the launch traced here: 46.7 us
  Pallas kernels  44.7 us (95%)
  local copies, waits for them, and re-layouts  1.97 us (4%)
    pallas_call x1, Pallas kernels, local(): pl.pallas_call(kernel, out_shape=jax.ShapeDtypeStruct(tracers.shape, f32)...  44.7 us
    unnamed x1, local copies, waits for them, and re-layouts  1.97 us

profile of v4, /device:TPU:1, one launch (start us, length us, event | category | flops | bytes accessed | tf_op | source)
XLA Modules:
  0.0 46.7 jit_solution(6176997438545721586)
XLA Ops:
  0.0 44.7 %shard_map.100 = f32[10,8,16,128]{3,2,1,0:T(8,128)} custom-call(f32[10,8,16,128]{3,2,1,0:T(8,128)} %x_ref.1, f32[2,1,16,128]{3,2,1,0:T(8,128)} %c_ref.1, s32[1,80]{1,0:T(1,128)} %bitcast.7, f32[1,80]{1,0:T(1,128)} %bitcast.8, bf16[80,256]{1,0:T(8,128)(2,1)} %bitcast.5, f32[1,256]{1,0:T(1,128)} %bitcast.6, bf16[2,256,256]{2,1,0:T(8,128)(2,1)} %wmid_ref.1, ...), custom_call_target="tpu_custom_call" | custom-call | flops 704000000 | bytes 4000000 | tf_op jit(solution)/shard_map/pallas_call | solution.py:447
  44.7 2.0 %copy.12 = f32[10,8,16,128]{3,2,1,0:T(8,128)} copy(f32[10,8,16,128]{3,2,1,0:T(8,128)} %shard_map.100) | data formatting | bytes 1310720

commit v5 on v4

--- a/solution.py
+++ b/solution.py
@@ -9,9 +9,9 @@
 
 MESH = pl.DeviceIdType.MESH
 VM = 60 * 1024 * 1024
-GROUPS = (2, 3, 4, 4, 3)
-STARTS_EVEN = (11, 13, 7, 3, 0)
-STARTS_ODD = (3, 0, 5, 9, 13)
+GROUPS = (2, 3, 2, 6, 3)
+STARTS_EVEN = (11, 13, 9, 3, 0)
+STARTS_ODD = (3, 0, 5, 7, 13)
 
 
 def upwind(f):
@@ -77,18 +77,18 @@
 
     c1h[...] = jnp.zeros((2, 8, 128), jnp.float32)
     barrier = pltpu.get_barrier_semaphore()
+    first = lax.rem(x, 2) == 0
+
+    @pl.when(first)
+    def _():
+        for side in (left, right):
+            for k in range(8):
+                pl.semaphore_signal(barrier, inc=1, device_id={"trc": k, **side}, device_id_type=MESH)
+
     for d in range(1, 8):
         pl.semaphore_signal(barrier, inc=1, device_id={"trc": peer(d)}, device_id_type=MESH)
     for d in (1, 3):
         pl.semaphore_signal(barrier, inc=1, device_id={"ty": lax.rem(y + d, 4)}, device_id_type=MESH)
-
-    first = lax.rem(x, 2) == 0
-
-    @pl.when(first)
-    def _():
-        for side in (left, right):
-            for k in range(8):
-                pl.semaphore_signal(barrier, inc=1, device_id={"trc": k, **side}, device_id_type=MESH)
 
     lane8 = lax.broadcasted_iota(jnp.int32, (8, 128), 1)
     lane16 = lax.broadcasted_iota(jnp.int32, (16, 128), 1)
@@ -141,13 +141,13 @@
                 v = pltpu.roll(xv2[pl.ds(g * 128 + 8 * h + i, 8, stride=16), :], (16 * i + 8) % 128, 1)
                 part[h] = jnp.where(lane8 // 16 == i, v, part[h])
         q = jnp.where(at16 < 8, pltpu.roll(part[1], 125, 1), pltpu.roll(part[1], 3, 1))
-        q_out[pl.ds(pl.multiple_of(g * 8, 8), 8), :] = jnp.where((at16 >= 5) & (at16 <= 10), part[0], q)
-
-    q_out3 = q_out.reshape(10, 8, 128)
+        q_out[pl.ds(g, 8, stride=16), :] = jnp.where((at16 >= 5) & (at16 <= 10), part[0], q)
+
+    q_out3 = q_out.reshape(8, 16, 128)
 
     def edges(side, k):
         return remote(
-            q_out3.at[:, k], q_in.at[1 - side, pl.ds(10 * me, 10)], qs.at[side, k], qr.at[1 - side, me],
+            q_out3.at[k, pl.ds(0, 10)], q_in.at[1 - side, pl.ds(10 * me, 10)], qs.at[side, k], qr.at[1 - side, me],
             {"trc": k, **(left, right)[side]},
         )
 
@@ -314,7 +314,7 @@
         n = GROUPS[p]
         start = STARTS_ODD[p] + even * (STARTS_EVEN[p] - STARTS_ODD[p])
 
-        @pl.loop(0, 10)
+        @pl.loop(0, 10, unroll=2)
         def _(g):
             at = pl.ds(pl.multiple_of(g * 8, 8), 8)
             s = [swept[start + t, at, :] for t in range(n + 6)]
@@ -432,9 +432,9 @@
         w_mid, b_mid, w_out, b_out.reshape(1, 80),
     )
     scratch = [
-        ((10, 8, 16, 128), f32), ((2, 80, 8, 128), f32), ((22, 80, 128), f32), ((2, 80, 128), f32), ((80, 128), f32), ((5, 80, 128), f32),
+        ((10, 8, 16, 128), f32), ((2, 80, 8, 128), f32), ((22, 80, 128), f32), ((2, 80, 128), f32), ((80, 128), f32), ((8, 80, 128), f32),
         ((5, 80, 8, 128), f32), ((2, 16, 128), f32), ((2, 8, 128), f32), ((8, 128), f32), ((8, 128), f32),
-        ((8, 128), f32), ((80, 128), f32), ((2, 80, 128), f32), ((16, 8, 128), f32), ((17, 8, 128), f32),
+        ((8, 128), f32), ((128, 128), f32), ((2, 80, 128), f32), ((16, 8, 128), f32), ((17, 8, 128), f32),
         ((2, 2, 8, 128), f32),
         ((1, 80), jnp.int32), ((1, 80), f32), ((80, 256), bf16), ((1, 256), f32), ((2, 256, 256), bf16),
         ((2, 256), f32), ((80, 256), bf16), ((1, 80), f32),

time: 46.9 us -> 46.3 us (0.987)
  Pallas kernels: 44.7 us -> 44.1 us
    pallas_call x1, Pallas kernels: 44.7 us -> 44.1 us  [local(): pl.pallas_call(kernel, out_shape=jax.ShapeDtypeStruct(tracers.shape, f32)...]
where the time goes in v5:
time: 46.3 us; the launch traced here: 46.1 us
  Pallas kernels  44.1 us (95%)
  local copies, waits for them, and re-layouts  1.97 us (4%)
    pallas_call x1, Pallas kernels, local(): pl.pallas_call(kernel, out_shape=jax.ShapeDtypeStruct(tracers.shape, f32)...  44.1 us
    unnamed x1, local copies, waits for them, and re-layouts  1.97 us

profile of v5, /device:TPU:1, one launch (start us, length us, event | category | flops | bytes accessed | tf_op | source)
XLA Modules:
  0.0 46.1 jit_solution(2794228198099123877)
XLA Ops:
  0.0 44.1 %shard_map.100 = f32[10,8,16,128]{3,2,1,0:T(8,128)} custom-call(f32[10,8,16,128]{3,2,1,0:T(8,128)} %x_ref.1, f32[2,1,16,128]{3,2,1,0:T(8,128)} %c_ref.1, s32[1,80]{1,0:T(1,128)} %bitcast.7, f32[1,80]{1,0:T(1,128)} %bitcast.8, bf16[80,256]{1,0:T(8,128)(2,1)} %bitcast.5, f32[1,256]{1,0:T(1,128)} %bitcast.6, bf16[2,256,256]{2,1,0:T(8,128)(2,1)} %wmid_ref.1, ...), custom_call_target="tpu_custom_call" | custom-call | flops 704000000 | bytes 4000000 | tf_op jit(solution)/shard_map/pallas_call | solution.py:447
  44.2 2.0 %copy.12 = f32[10,8,16,128]{3,2,1,0:T(8,128)} copy(f32[10,8,16,128]{3,2,1,0:T(8,128)} %shard_map.100) | data formatting | bytes 1310720

commit v6 on v5

--- a/solution.py
+++ b/solution.py
@@ -49,11 +49,11 @@
 
 def kernel(
     x_ref, c_ref, as_ref, gain_ref, win_ref, bin_ref, wmid_ref, bmid_ref, wout_ref, bout_ref,
-    o_ref,
+    o_ref, b_ref,
     xv, got, swept, strip, fixed, adv, back, cv, c1h, eco, ecl, ecr, q_out, q_in, cc, cf, sc,
     v_as, v_gain, v_win, v_bin, v_wmid, v_bmid, v_wout, v_bout,
     first_w, last_w, bias_b, last_b, gain_b,
-    fs, fr, fl, lw, qs, qr, ready, es, er, c1s, c1r, hs, hr, os_, or_, ol,
+    fs, fr, fl, lw, qs, qr, ready, es, er, c1s, c1r, hs, hr, os_, or_, ol, bl,
 ):
     me, y, x = lax.axis_index("trc"), lax.axis_index("ty"), lax.axis_index("tx")
     even = 1 - lax.rem(y, 2)
@@ -214,6 +214,8 @@
     last_w[...] = jnp.dot(pick, v_wout[...], preferred_element_type=jnp.float32).astype(jnp.bfloat16)
     gain_b[...] = jnp.broadcast_to(jnp.sum(jnp.where(chosen, v_gain[...], 0.0), axis=1, keepdims=True), (80, 128))
     last_b[...] = jnp.broadcast_to(jnp.sum(jnp.where(chosen, v_bout[...], 0.0), axis=1, keepdims=True), (80, 128))
+    own_bias = pltpu.make_async_copy(last_b.at[pl.ds(10 * me, 10)], b_ref, bl)
+    own_bias.start()
     bias_b[0] = jnp.broadcast_to(column_of(v_bin[...], 256), (256, 128))
     bias_b[1] = jnp.broadcast_to(column_of(v_bmid[0:1, :], 256), (256, 128))
     bias_b[2] = jnp.broadcast_to(column_of(v_bmid[1:2, :], 256), (256, 128))
@@ -339,7 +341,7 @@
             h = gelu(jnp.dot(v_wmid[m], h, preferred_element_type=jnp.float32) + wide(bias_b[m + 1]))
         tend = jnp.dot(last_w[...], h, preferred_element_type=jnp.float32)
         for t in range(n):
-            back2[p][pl.ds(t, 80, stride=8), :] = adv[t] + (tend[:, 128 * t : 128 * t + 128] + last_b[...])
+            back2[p][pl.ds(t, 80, stride=8), :] = adv[t] + tend[:, 128 * t : 128 * t + 128]
         rows = pl.ds(start, n)
         for d in range(1, 8):
             k = peer(d)
@@ -420,6 +422,7 @@
     for p in range(2):
         for d in range(1, 8):
             forward(p, d).wait_send()
+    own_bias.wait()
     for p in range(5):
         finish(p)
 
@@ -442,19 +445,20 @@
     ]
     semaphores = [
         dma((2, 8)), dma((2, 8)), dma((2,)), dma((10,)), dma((2, 8)), dma((2, 8)), pltpu.SemaphoreType.REGULAR((2,)),
-        dma((2,)), dma((2,)), dma((2,)), dma((2,)), dma((2,)), dma((2,)), dma((5, 8)), dma((5, 8)), dma((5,)),
+        dma((2,)), dma((2,)), dma((2,)), dma((2,)), dma((2,)), dma((2,)), dma((5, 8)), dma((5, 8)), dma((5,)), pltpu.SemaphoreType.DMA,
     ]
-    return pl.pallas_call(
+    result, bias = pl.pallas_call(
         kernel,
-        out_shape=jax.ShapeDtypeStruct(tracers.shape, f32),
+        out_shape=(jax.ShapeDtypeStruct(tracers.shape, f32), jax.ShapeDtypeStruct((10, 128), f32)),
         in_specs=[pl.BlockSpec(memory_space=pl.ANY)] * len(operands),
-        out_specs=pl.BlockSpec(memory_space=pl.ANY),
+        out_specs=[pl.BlockSpec(memory_space=pl.ANY)] * 2,
         scratch_shapes=[pltpu.VMEM(*s) for s in scratch] + semaphores,
         compiler_params=pltpu.CompilerParams(
             collective_id=0, has_side_effects=True, vmem_limit_bytes=VM
         ),
         cost_estimate=pl.CostEstimate(flops=704_000_000, bytes_accessed=4_000_000, transcendentals=1_600_000),
     )(*operands)
+    return result + bias[:, None, None, :]
 
 
 def solution(mesh):

time: 46.3 us -> 46.3 us (level)
  other arithmetic: 0 us -> 1.99 us
  local copies, waits for them, and re-layouts: 1.97 us -> 0 us
    add x0 -> x1, other arithmetic: none -> 1.99 us  [local(): return result + bias[:, None, None, :]]
    unnamed x1 -> x0, local copies, waits for them, and re-layouts: 1.97 us -> none
where the time goes in v6:
time: 46.3 us; the launch traced here: 46.2 us
  Pallas kernels  44.2 us (95%)
  other arithmetic  1.99 us (4%)
    pallas_call x1, Pallas kernels, local(): pl.pallas_call(kernel, out_shape=(jax.ShapeDtypeStruct(tracers.shape, f32...  44.2 us
    add x1, other arithmetic, local(): return result + bias[:, None, None, :]  1.99 us

profile of v6, /device:TPU:1, one launch (start us, length us, event | category | flops | bytes accessed | tf_op | source)
XLA Modules:
  0.0 46.2 jit_solution(16599884835401481992)
XLA Ops:
  0.0 44.2 %shard_map.100 = (f32[10,8,16,128]{3,2,1,0:T(8,128)}, f32[10,128]{1,0:T(8,128)}) custom-call(f32[10,8,16,128]{3,2,1,0:T(8,128)} %x_ref.1, f32[2,1,16,128]{3,2,1,0:T(8,128)} %c_ref.1, s32[1,80]{1,0:T(1,128)} %bitcast.7, f32[1,80]{1,0:T(1,128)} %bitcast.8, bf16[80,256]{1,0:T(8,128)(2,1)} %bitcast.5, f32[1,256]{1,0:T(1,128)} %bitcast.6, ...), custom_call_target="tpu_custom_call" | custom-call | flops 704000000 | bytes 4000000 | tf_op jit(solution)/shard_map/pallas_call | solution.py:450
  44.2 2.0 %broadcast_add_fusion = f32[10,8,16,128]{3,2,1,0:T(8,128)} fusion(f32[10,8,16,128]{3,2,1,0:T(8,128)} %get-tuple-element.7, f32[10,128]{1,0:T(8,128)} %get-tuple-element.8), kind=kLoop, calls=%fused_computation | loop fusion | flops 163840 | bytes 1315840 | tf_op jit(solution)/shard_map/add | solution.py:461
